TPU v7x, 256 devices: a whole 4x4x8 slice. The times are simulated.
256 devices in a mesh: group: 8 (over x, core), fsdp: 32 (over z, y).
Axes of the slice: x: 4, y: 4, z: 8, core: 2. Of those that a mesh axis runs over, the one named last changes fastest.
Arguments:
- resid_in: bfloat16 [512, 320, 1536], P(('group', 'fsdp')), may hold values from -44 to 44
- attn_out: bfloat16 [512, 320, 1536], P(('group', 'fsdp')), may hold values from -6 to 6
- target_rows: bfloat16 [512, 320, 1536], P(('group', 'fsdp')), may hold values from -6 to 6
- out_weight: bfloat16 [1536, 1536], P('fsdp'), may hold values from -0.15625 to 0.15625
- norm_gain: bfloat16 [1536], replicated, may hold values from 0.099609375 to 1.8984375
- seq_lengths: int32 [512], replicated, may hold values from 33 to 320, as said below
- prompt_ids: int32 [512], replicated, may hold values from 0 to 63, as said below
- log_offsets: float32 [512], replicated, may hold values from -48 to 57
- plan_dest: int32 [512, 5], replicated, may hold values from -1 to 7, as said below
- plan_slot: int32 [512, 5], replicated, may hold values from -1 to 5, as said below
Outputs:
- resid_grad: bfloat16 [512, 320, 1536], P(('group', 'fsdp'))
- attn_grad: bfloat16 [512, 320, 1536], P(('group', 'fsdp'))
- weight_grad: float32 [1536, 1536], P('fsdp')
- loss: float32 [], replicated
Inputs may be any that keep to these rules, and one draw needn't show every extreme that they name: `seq_lengths`: A sequence of length l covers its first ceil(l / 64) buckets; the sequences of one index of fsdp cover exactly 48 buckets together, and on every index of fsdp some device has all 2 sequences of length 320. `plan_dest`: -1 exactly for buckets that the sequence doesn't cover. Among the devices of one index of fsdp, each works on exactly 6 buckets, and no device sends more than 2 of its buckets to one device; some device sends exactly 2 to one device. `plan_slot`: -1 where plan_dest is -1. For one index of fsdp, every pair of working device and position below 6 is taken by exactly one bucket. `prompt_ids`: the sequences of index g along group (g * 2 * 32 onwards) belong to prompts g * 8 to g * 8 + 7, each prompt with exactly 8 sequences.
All inputs are finite; a program needn't handle non-finite values.
Results may differ from a plain program's by a relative error of at most 0.005.
Values may be sent and summed in bfloat16 or wider, within the bound.
A program may use at most 128 MiB of HBM per device.

v0:
```python
import math

import jax
import jax.numpy as jnp
from jax import lax
from jax.sharding import PartitionSpec as P

PPG = 8


EPS = 1e-06


def forward_rows(x_rows, o_rows, e_rows, weight, gain, mask):
    width = x_rows.shape[-1]
    mixed = x_rows.astype(jnp.float32) + jnp.dot(o_rows, weight, preferred_element_type=jnp.float32)
    scale_inv = lax.rsqrt(jnp.mean(mixed * mixed, axis=-1, keepdims=True) + EPS)
    normed = mixed * scale_inv * gain.astype(jnp.float32)
    token_logp = jnp.sum(normed * e_rows.astype(jnp.float32), axis=-1) * mask / math.sqrt(width)
    return (mixed, scale_inv, token_logp)


def backward_rows(mixed, scale_inv, e_rows, gain, coeff, weight):
    width = mixed.shape[-1]
    gained = (
        coeff[:, None] * e_rows.astype(jnp.float32) * gain.astype(jnp.float32) / math.sqrt(width)
    )
    inner = jnp.mean(mixed * gained, axis=-1, keepdims=True)
    grad_rows = (scale_inv * gained - mixed * scale_inv**3 * inner).astype(jnp.bfloat16)
    attn_rows = lax.dot_general(
        grad_rows, weight, (((1,), (1,)), ((), ())), preferred_element_type=jnp.float32
    ).astype(jnp.bfloat16)
    return (grad_rows, attn_rows)


def local(
    resid_in,
    attn_out,
    target_rows,
    out_weight,
    norm_gain,
    seq_lengths,
    prompt_ids,
    log_offsets,
    plan_dest,
    plan_slot,
):
    seq_dev, lmax, width = resid_in.shape
    n_group = lax.axis_size("group")
    n_fsdp = lax.axis_size("fsdp")
    group_idx = lax.axis_index("group")
    fsdp_idx = lax.axis_index("fsdp")
    total_seqs = seq_lengths.shape[0]
    prompts = PPG * n_group
    samples = seq_dev * n_fsdp // PPG
    prompt_range = jnp.arange(prompts, dtype=jnp.int32)
    weight = lax.all_gather(out_weight, "fsdp", axis=0, tiled=True)
    first = (group_idx * n_fsdp + fsdp_idx) * seq_dev
    my_len = lax.dynamic_slice_in_dim(seq_lengths, first, seq_dev)
    positions = jnp.arange(lmax, dtype=jnp.int32)
    mask = (positions[None, :] < my_len[:, None]).astype(jnp.float32).reshape(-1)
    x_rows = resid_in.reshape(-1, width)
    o_rows = attn_out.reshape(-1, width)
    e_rows = target_rows.reshape(-1, width)
    mixed, scale_inv, token_logp = forward_rows(x_rows, o_rows, e_rows, weight, norm_gain, mask)
    seq_logp = jnp.sum(token_logp.reshape(seq_dev, lmax), axis=1)
    delta = seq_logp + lax.dynamic_slice_in_dim(log_offsets, first, seq_dev)
    my_prompt = lax.dynamic_slice_in_dim(prompt_ids, first, seq_dev)
    member = (my_prompt[:, None] == prompt_range[None, :]).astype(jnp.float32)
    prompt_part = jnp.sum(member * delta[:, None], axis=0)
    prompt_total = lax.psum(prompt_part, "fsdp")
    baseline = prompt_total / samples
    centred = delta - jnp.sum(member * baseline[None, :], axis=1)
    square_total = lax.psum(jnp.sum(centred * centred), ("group", "fsdp"))
    coeff = jnp.repeat(centred, lmax) * mask
    grad_rows, attn_rows = backward_rows(mixed, scale_inv, e_rows, norm_gain, coeff, weight)
    resid_grad = grad_rows.reshape(seq_dev, lmax, width)
    attn_grad = attn_rows.reshape(seq_dev, lmax, width)
    part_rows = lax.psum_scatter(
        lax.dot_general(
            o_rows, grad_rows, (((0,), (0,)), ((), ())), preferred_element_type=jnp.float32
        ),
        "fsdp",
        scatter_dimension=0,
        tiled=True,
    )
    weight_grad = lax.psum(part_rows, "group") / total_seqs
    loss = square_total / (total_seqs * lmax)
    return (resid_grad, attn_grad, weight_grad, loss)


def solution(mesh):
    return jax.shard_map(
        local,
        mesh=mesh,
        in_specs=(
            P(("group", "fsdp"), None, None),
            P(("group", "fsdp"), None, None),
            P(("group", "fsdp"), None, None),
            P("fsdp", None),
            P(),
            P(),
            P(),
            P(),
            P(),
            P(),
        ),
        out_specs=(
            P(("group", "fsdp"), None, None),
            P(("group", "fsdp"), None, None),
            P("fsdp", None),
            P(),
        ),
        check_vma=False,
    )
```

profile of v0, /device:TPU:1, one launch (start us, length us, event | category | flops | bytes accessed | tf_op | source)
XLA Modules:
  0.0 528.0 jit_solution(14675733992348107023)
XLA Ops:
  7.2 0.0 copy-start
  7.2 0.0 all-gather.2.cloned.1.call-start
  7.2 0.7 all-gather.2.cloned.1.call-update
  7.9 0.0 reduce-scatter.4.cloned.1.call-start
  8.0 0.8 dynamic_slice.9
  8.7 0.8 dynamic_slice.11
  9.5 0.7 convert_element_type.30
  10.2 85.1 %all-gather.2.cloned.1.call-done = bf16[1536,1536]{1,0:T(8,128)(2,1)} async-done(((bf16[48,1536]{1,0:T(8,128)(2,1)}), bf16[1536,1536]{1,0:T(8,128)(2,1)}) %all-gather.2.cloned.1.call-update) | async-done | bytes 4718608 | tf_op jit(solution)/shard_map/all_gather | solution.py:57
  95.2 0.0 copy-done
  95.2 0.0 copy-start.3
  95.2 6.4 %multiply_reduce_fusion = (f32[640]{0:T(1024)S(1)}, f32[640,1536]{1,0:T(8,128)S(1)}) fusion(bf16[640,1536]{1,0:T(8,128)(2,1)S(1)} %bitcast.19, bf16[1536,1536]{1,0:T(8,128)(2,1)} %all-gather.2.cloned.1.call-done, bf16[640,1536]{1,0:T(8,128)(2,1)} %bitcast.22), kind=kOutput, calls=%fused_computation.12 | convolution fusion | flops 3023830528 | bytes 12585472 | tf_op jit(solution)/shard_map/dot_general | solution.py:16
  101.7 0.0 copy-start.1
  101.7 1.9 copy-done.1
  103.5 0.0 copy-done.3
  103.5 0.8 fusion
  104.3 0.1 reduce_sum.67
  104.4 0.2 multiply_reduce_fusion.1
  104.6 0.8 dynamic-slice_add_fusion
  105.4 0.1 select_reduce_fusion.1
  105.4 57.6 %psum.21 = f32[64]{0:T(128)S(1)} all-reduce(f32[64]{0:T(128)S(1)} %select_reduce_fusion.1), channel_id=1, replica_groups=mesh['group'=8,'fsdp'=32] {'fsdp'}, use_global_device_ids=true, to_apply=%region_4.0 | all-reduce | flops 64 | bytes 512 | tf_op jit(solution)/shard_map/psum | solution.py:71
  163.0 0.2 select_reduce_fusion
  163.2 0.6 multiply_reduce_fusion.2
  163.8 0.1 fusion.8
  163.9 0.1 mul.116
  163.9 0.0 copy-start.2
  163.9 0.0 copy-start.4
  164.0 3.8 fusion.7
  167.7 0.1 copy-done.2
  167.8 0.6 copy-done.4
  168.4 1.2 fusion.5
  169.7 0.0 copy-start.5
  169.7 1.3 copy-done.5
  170.9 6.3 %convolution_bitcast_fusion = f32[1536,1536]{0,1:T(8,128)} fusion(bf16[640,1536]{1,0:T(8,128)(2,1)S(1)} %fusion.5, bf16[640,1536]{1,0:T(8,128)(2,1)S(1)} %bitcast.20), kind=kOutput, calls=%fused_computation | convolution fusion | flops 3019898880 | bytes 13369344 | tf_op jit(solution)/shard_map/dot_general | solution.py:80
  177.2 9.6 %copy.15 = f32[1536,1536]{1,0:T(8,128)} copy(f32[1536,1536]{0,1:T(8,128)} %convolution_bitcast_fusion) | data formatting | bytes 18874368
  186.9 0.0 reduce-scatter.4.cloned.1.call-update
  186.9 0.0 all-reduce.2.cloned.1.call-start
  187.0 242.0 %reduce-scatter.4.cloned.1.call-done = f32[48,1536]{1,0:T(8,128)} async-done(((f32[1536,1536]{1,0:T(8,128)}), f32[48,1536]{1,0:T(8,128)}) %reduce-scatter.4.cloned.1.call-update) | async-done | bytes 294928
  429.0 2.1 copy.16
  431.1 0.0 all-reduce.2.cloned.1.call-update
  431.1 7.5 %convolution_convert_fusion = bf16[640,1536]{1,0:T(8,128)(2,1)} fusion(bf16[640,1536]{1,0:T(8,128)(2,1)} %copy-done.5, bf16[1536,1536]{1,0:T(8,128)(2,1)} %all-gather.2.cloned.1.call-done), kind=kOutput, calls=%fused_computation.13 | convolution fusion | flops 3020881920 | bytes 8650752 | tf_op jit(solution)/shard_map/dot_general | solution.py:30
  438.6 78.9 %psum.23 = f32[]{:T(128)} all-reduce(f32[]{:T(128)} %get-tuple-element.16), channel_id=1, replica_groups=mesh['group'=8,'fsdp'=32] {'group','fsdp'}, use_global_device_ids=true, to_apply=%region_10.0 | all-reduce | flops 1 | bytes 8 | tf_op jit(solution)/shard_map/psum | solution.py:74
  518.1 0.0 all-reduce.2.cloned.1.call-done
  518.1 1.2 broadcast_multiply_fusion
  519.3 1.0 copy.14
  (3 shorter events, 0.0 us)
Async XLA Ops:
  7.2 88.1 %copy-start = (bf16[2,320,1536]{2,1,0:T(8,128)(2,1)S(1)}, bf16[2,320,1536]{2,1,0:T(8,128)(2,1)}, u32[]{:S(2)}) copy-start(bf16[2,320,1536]{2,1,0:T(8,128)(2,1)} %param.11) | copy-start | bytes 5898244
  7.2 88.1 %all-gather.2.cloned.1.call-start = ((), (), s32[]{:S(2)}) async-start(), calls=%async_computation.1 | async-start | bytes 4866048 | tf_op jit(solution)/shard_map/all_gather | solution.py:57
  7.9 421.1 %reduce-scatter.4.cloned.1.call-start = ((), (), s32[]{:S(2)}) async-start(), calls=%async_computation.3 | async-start | bytes 9732096
  95.2 8.3 %copy-start.3 = (bf16[2,320,1536]{2,1,0:T(8,128)(2,1)S(1)}, bf16[2,320,1536]{2,1,0:T(8,128)(2,1)}, u32[]{:S(2)}) copy-start(bf16[2,320,1536]{2,1,0:T(8,128)(2,1)} %param.12) | copy-start | bytes 5898244
  101.7 1.9 copy-start.1
  163.9 3.9 copy-start.2
  163.9 4.5 copy-start.4
  169.7 1.3 copy-start.5
  186.9 331.2 %all-reduce.2.cloned.1.call-start = ((), (), s32[]{:S(2)}) async-start(), calls=%async_computation.2 | async-start | bytes 1572864 | tf_op jit(solution)/shard_map/psum | solution.py:87
Sparse Core Ops, SparseCore 0:
  10.6 84.6 all-gather.1
  187.0 241.9 reduce-scatter.3
  431.3 67.3 all-reduce.1
where the time goes:
time: 528 us
  waiting for transfers between devices  328 us (62%)
  blocking collectives  136 us (26%)
  matrix products  20.2 us (4%)
  local copies, waits for them, and re-layouts  18.2 us (3%)
  between operations  15.6 us (3%)
  other arithmetic  9.56 us (2%)
    unnamed x4, waiting for transfers between devices  243 us
    all_gather x1, waiting for transfers between devices, local(): weight = lax.all_gather(out_weight, 'fsdp', axis=0, tiled=True)  85.1 us
    psum x1, blocking collectives, local(): square_total = lax.psum(jnp.sum(centred * centred), ('group', 'fsdp'))  78.9 us
    psum x1, blocking collectives, local(): prompt_total = lax.psum(prompt_part, 'fsdp')  57.6 us
    unnamed x15, local copies, waits for them, and re-layouts  16.5 us
  transfers between devices with their start and end apart: 3, of which 2 were waited for; matrix products, arithmetic and copies ran while one was open for 2% of the time, Pallas kernels for 0%

commit v1 on v0

v1 whole, which is shorter than its diff:
```python
import functools
import math

import jax
import jax.numpy as jnp
from jax import lax
from jax.experimental import pallas as pl
from jax.experimental.pallas import tpu as pltpu
from jax.sharding import PartitionSpec as P

MESH = pl.DeviceIdType.MESH
F32, BF16 = jnp.float32, jnp.bfloat16
NX, NC, NZ, NY = 4, 2, 8, 4
EPS = 1e-06
PPG = 8
SAMPLES = 8
D = 1536
TOK = 640
SEQ = 320
H = D // 2
Q = D // 4
RB = 48

Z_ARRIVE = (0, -1, 1, -2, 2, -3, 3, -4)
Y_ARRIVE = (0, -1, 1, -2)
Z_LEAVE = (4, -3, 3, -2, 2, -1, 1, 0)
Y_LEAVE = (2, -1, 1, 0)


class Op:
    def __init__(self, key, waits=(), after=(), sends=(), cost=0.1, rank=0):
        self.key, self.waits, self.after, self.sends, self.cost, self.rank = key, waits, after, sends, cost, rank


def order(ops, size):
    now, done, at, free, out = 0.0, set(), {}, {"z": 0.0, "y": 0.0}, []
    left = list(ops)
    while left:
        best = None
        for n, op in enumerate(left):
            if all(a in done for a in op.after) and all(w in at for w in op.waits):
                ready = max([now] + [at[w] for w in op.waits])
                score = (ready, op.rank, n)
                if best is None or score < best[0]:
                    best = (score, op)
        (ready, _, _), op = best
        left.remove(op)
        now = ready + op.cost
        for axis, event in op.sends:
            start = max(now, free[axis])
            free[axis] = start + size(event)
            at[event] = free[axis] + 1.5
        done.add(op.key)
        out.append(op)
    return out


def gather_ops():
    ops = []

    def a_first(off):
        sends = [("y", ("Ay", "L", 1, off)), ("y", ("Ay", "S", 1, off))]
        if off <= 0 and off > -4:
            sends.insert(0, ("z", ("Az", "L", 1 - off)))
        if off >= 0 and off < 3:
            sends.insert(0, ("z", ("Az", "S", off + 1)))
        return sends

    def b_first(off):
        sends = [("z", ("Bz", "L", 1, off)), ("z", ("Bz", "S", 1, off))]
        if off <= 0 and off > -2:
            sends.insert(0, ("y", ("By", "L", 1 - off)))
        if off == 0:
            sends.insert(0, ("y", ("By", "S", 1)))
        return sends

    ops.append(Op("start", sends=b_first(0) + a_first(0)))
    for off in Z_ARRIVE[1:]:
        event = ("Az", "L" if off < 0 else "S", abs(off))
        ops.append(Op(event, waits=[event], after=["start"], sends=a_first(off)))
    for off in Y_ARRIVE[1:]:
        event = ("By", "L" if off < 0 else "S", abs(off))
        ops.append(Op(event, waits=[event], after=["start"], sends=b_first(off)))
    for off in Z_ARRIVE:
        for d, k, last in (("L", 1, 2), ("L", 2, 2), ("S", 1, 1)):
            event = ("Ay", d, k, off)
            sends = [("y", ("Ay", d, k + 1, off))] if k < last else []
            ops.append(Op(event, waits=[event], after=["start"], sends=sends))
    for off in Y_ARRIVE:
        for d, last in (("L", 4), ("S", 3)):
            for k in range(1, last + 1):
                event = ("Bz", d, k, off)
                sends = [("z", ("Bz", d, k + 1, off))] if k < last else []
                ops.append(Op(event, waits=[event], after=["start"], sends=sends))
    return ops


def scatter_ops():
    ops = []
    for n, yo in enumerate(Y_LEAVE):
        sends = []
        if n == 0:
            sends = [("y", ("Ay", "L", 1, i)) for i in range(8)]
        if n == 1:
            sends = [("y", ("Ay", "S", 1, i)) for i in range(8)]
        ops.append(Op(("CA", n), sends=sends, cost=0.6, rank=2 + n))
    for i, zo in enumerate(Z_LEAVE):
        sends = []
        if i == 0:
            sends = [("z", ("Bz", "L", 1, j)) for j in range(4)]
        if i == 1:
            sends = [("z", ("Bz", "S", 1, j)) for j in range(4)]
        ops.append(Op(("CB", i), sends=sends, cost=0.35, rank=2 + i / 2))
    for i in range(8):
        ops.append(Op(("FA", i), waits=[("Ay", "L", 1, i)], after=[("CA", 0), ("CA", 2)], sends=[("y", ("Ay", "L", 2, i))]))
        waits = [("Ay", "L", 2, i), ("Ay", "S", 1, i)]
        sends = []
        if i >= 2:
            waits.append(("Az", "LS"[i % 2], i // 2) if i < 7 else ("Az", "S", 3))
        if i == 7:
            waits.append(("Az", "L", 4))
        else:
            sends = [("z", ("Az", "LS"[i % 2], i // 2 + 1))]
        ops.append(Op(("TA", i), waits=waits, after=[("CA", 3)], sends=sends))
    for i in range(2, 8):
        for j in range(4):
            if i < 7:
                waits = [("Bz", "LS"[i % 2], i // 2, j)]
                sends = [("z", ("Bz", "LS"[i % 2], i // 2 + 1, j))]
            else:
                waits = [("Bz", "L", 4, j), ("Bz", "S", 3, j)]
                sends = [("y", ("By", "L", 1)), ("y", ("By", "S", 1)), ("y", ("By", "L", 2)), None][j]
                sends = [sends] if sends else []
                if j == 2:
                    waits.append(("By", "L", 1))
                if j == 3:
                    waits += [("By", "L", 2), ("By", "S", 1)]
            ops.append(Op(("FB", i, j), waits=waits, after=[("CB", i)], sends=sends))
    ops.append(Op("loss", after=[("CA", 3), ("CB", 7)], cost=1.0, rank=20))
    for n in range(4):
        ops.append(Op(("attn", n), after=[("CA", 3), ("CB", 7)], cost=1.2, rank=30 + n))
    return ops


GATHER = order(gather_ops(), lambda e: 0.4)
SCATTER = order(scatter_ops(), lambda e: 0.8 if e[0] in ("Az", "By") else 0.4)
G_ID = {e: n for n, e in enumerate(e for op in GATHER for _, e in op.sends)}
S_ID = {e: n for n, e in enumerate(e for op in SCATTER for _, e in op.sends)}


def kernel(
    x_hbm, o_hbm, e_hbm, w_hbm, gain_ref, len_ref, pid_ref, off_ref, prow_ref,
    rg_hbm, ag_hbm, wg_ref, loss_ref,
    wbuf, xb, ob, eb, ot, mixed, ss_ref, t_ref, g, gall, attn,
    da, db, sa, ra, sa2, ra2, sb, rb, sb2, rb2,
    fin, xr, xg, sg, my, mz, msg1, msg2, ls, lx, lmsg1, lmsg2, crow,
    loc, g_send, g_recv, b_send, b_recv, o_send, o_recv, h_send, h_recv, r_send, r_recv,
    y_send, y_recv, z_send, z_recv, x_send, x_recv, w_send, w_recv, c_send, c_recv, l_send, l_recv, m_send, m_recv,
):
    gi, fi = lax.axis_index("group"), lax.axis_index("fsdp")
    x, c = gi // 2, lax.rem(gi, 2)
    z, y = fi // 4, lax.rem(fi, 4)
    s = 1 - 2 * c

    def zat(off):
        return lax.rem(z + off * s + 2 * NZ, NZ)

    def yat(off):
        return lax.rem(y + off * s + 2 * NY, NY)

    def dev(xx, cc, zz, yy):
        return (xx * 2 + cc, zz * 4 + yy)

    peer = {
        ("z", "L"): dev(x, c, zat(1), y),
        ("z", "S"): dev(x, c, zat(-1), y),
        ("y", "L"): dev(x, c, z, yat(1)),
        ("y", "S"): dev(x, c, z, yat(-1)),
    }
    sibling = dev(x, 1 - c, z, y)
    xs = [lax.rem(x + k, NX) for k in range(1, NX)]
    ys = [lax.rem(y + k, NY) for k in range(1, NY)]
    zs = [lax.rem(z + k, NZ) for k in range(1, NZ)]

    def remote(src, dst, send, recv, to):
        return pltpu.make_async_remote_copy(
            src_ref=src, dst_ref=dst, send_sem=send, recv_sem=recv, device_id=to, device_id_type=MESH
        )

    sent = []

    def start(copy):
        copy.start()
        sent.append(copy)

    loads = [
        pltpu.make_async_copy(w_hbm.at[:, 0:H], wbuf.at[0, z, y], loc.at[0]),
        pltpu.make_async_copy(w_hbm.at[:, H:D], wbuf.at[1, z, y], loc.at[1]),
        pltpu.make_async_copy(o_hbm, ob, loc.at[2]),
        pltpu.make_async_copy(x_hbm, xb, loc.at[3]),
        pltpu.make_async_copy(e_hbm, eb, loc.at[4]),
    ]
    for copy in loads:
        copy.start()

    barrier = pltpu.get_barrier_semaphore()
    greet = [sibling]
    greet += [dev(v, c, z, y) for v in xs] + [dev(x, c, z, v) for v in ys] + [dev(x, c, v, y) for v in zs]
    for to in greet:
        pl.semaphore_signal(barrier, inc=1, device_id=to, device_id_type=MESH)
    pl.semaphore_wait(barrier, len(greet))

    loads[0].wait()
    loads[1].wait()

    def block_of(event, sender):
        kind, d, k = event[:3]
        k = k - 1 if sender else k
        step = -k if d == "L" else k
        if kind == "Az":
            zz, yy = zat(step), y
        elif kind == "Ay":
            zz, yy = zat(event[3]), yat(step)
        elif kind == "By":
            zz, yy = z, yat(step)
        else:
            zz, yy = zat(step), yat(event[3])
        cols = pl.ds(0, Q) if kind[0] == "A" else pl.ds(Q, Q)
        return wbuf.at[c, zz, yy, :, cols], wbuf.at[1 - c, zz, yy, :, cols]

    def turn(n):
        piece = ob[:, pl.ds(n * Q, Q)].T
        ot[2 * n : 2 * n + 2, :, :, 0:TOK] = piece.reshape(2, 4, RB, TOK)
        part = ot.at[2 * n : 2 * n + 2, :, :, 0:TOK]
        start(remote(part, ot.at[2 * n : 2 * n + 2, :, :, TOK : 2 * TOK], o_send.at[n], o_recv.at[n], sibling))

    turn_at = {4: 0, 10: 1, 18: 2, 26: 3}
    for step, op in enumerate(GATHER):
        for event in op.waits:
            mine, _ = block_of(event, False)
            remote(mine, mine, g_send.at[G_ID[event]], g_recv.at[G_ID[event]], sibling).wait_recv()
        for axis, event in op.sends:
            blk, _ = block_of(event, True)
            start(remote(blk, blk, g_send.at[G_ID[event]], g_recv.at[G_ID[event]], peer[axis, event[1]]))
        for event in op.waits:
            mine, _ = block_of(event, False)
            start(remote(mine, mine, b_send.at[G_ID[event]], b_recv.at[G_ID[event]], sibling))
        if step == 0:
            loads[2].wait()
        if step in turn_at:
            turn(turn_at[step])
    for event, n in G_ID.items():
        kind, d, k = event[:3]
        step = k if d == "L" else -k
        if kind == "Az":
            zz, yy = zat(step), y
        elif kind == "Ay":
            zz, yy = zat(-event[3]), yat(step)
        elif kind == "By":
            zz, yy = z, yat(step)
        else:
            zz, yy = zat(step), yat(-event[3])
        cols = pl.ds(0, Q) if kind[0] == "A" else pl.ds(Q, Q)
        theirs = wbuf.at[1 - c, zz, yy, :, cols]
        remote(theirs, theirs, b_send.at[n], b_recv.at[n], sibling).wait_recv()
    loads[3].wait()
    loads[4].wait()

    def forward(m, _):
        rows = pl.ds(pl.multiple_of(m * 160, 160), 160)
        ss = jnp.zeros((160, 1), F32)
        tt = jnp.zeros((160, 1), F32)
        for h in range(2):
            cols = pl.ds(h * H, H)
            w = wbuf[h].reshape(D, H)
            acc = jnp.dot(ob[rows, :], w, preferred_element_type=F32) + xb[rows, cols].astype(F32)
            mixed[h, rows, :] = acc
            eg = eb[rows, cols].astype(F32) * gain_ref[:, cols].astype(F32)
            ss = ss + jnp.sum(acc * acc, axis=1, keepdims=True)
            tt = tt + jnp.sum(acc * eg, axis=1, keepdims=True)
        ss_ref[rows, :] = jnp.broadcast_to(ss, (160, 128))
        t_ref[rows, :] = jnp.broadcast_to(tt, (160, 128))
        return 0

    lax.fori_loop(0, TOK // 160, forward, 0)

    first = (gi * 32 + fi) * 2
    lane = lax.broadcasted_iota(jnp.int32, (8, 128), 1)
    pos = lax.broadcasted_iota(jnp.int32, (SEQ, 128), 0)
    root = 1.0 / math.sqrt(D)
    deltas = []
    for j in range(2):
        rows = pl.ds(j * SEQ, SEQ)
        mask = (pos < len_ref[first + j]).astype(F32)
        scale = lax.rsqrt(ss_ref[rows, :] * (1.0 / D) + EPS)
        t = t_ref[rows, :]
        logp = t * scale * mask * root
        deltas.append(jnp.broadcast_to(jnp.sum(logp, axis=0, keepdims=True), (8, 128)) + off_ref[first + j])
        ss_ref[rows, :] = scale * mask * root
        t_ref[rows, :] = -(scale * scale * scale) * mask * (t * (root / D))
    at = lax.rem(gi, 2) * 64 + 2 * fi
    msg1[...] = jnp.where(lane == at, deltas[0], jnp.where(lane == at + 1, deltas[1], 0.0))
    for k in range(3):
        start(remote(msg1, my.at[k], y_send.at[k], y_recv.at[k], dev(x, c, z, ys[k])))
    total = msg1[...]
    for k in range(3):
        remote(my.at[k], my.at[k], y_send.at[k], y_recv.at[k], sibling).wait_recv()
        total = total + my[k]
    msg2[...] = total
    for k in range(7):
        start(remote(msg2, mz.at[k], z_send.at[k], z_recv.at[k], dev(x, c, zs[k], y)))
    for k in range(7):
        remote(mz.at[k], mz.at[k], z_send.at[k], z_recv.at[k], sibling).wait_recv()
        total = total + mz[k]

    prow = jnp.broadcast_to(prow_ref[pl.ds(gi // 2, 1), :], (8, 128))
    for j in range(2):
        base = jnp.sum(jnp.where(prow == pid_ref[first + j], total, 0.0), axis=1, keepdims=True) * (1.0 / SAMPLES)
        crow[j] = deltas[j] - base

    def gradient(m, _):
        rows = pl.ds(pl.multiple_of(m * 64, 64), 64)
        cc = jnp.where(m < 5, crow[0], crow[1])[0:1]
        ga = ss_ref[rows, :] * cc
        gb = t_ref[rows, :] * cc
        ga = jnp.concatenate([ga] * 6, axis=1)
        gb = jnp.concatenate([gb] * 6, axis=1)
        for h in range(2):
            cols = pl.ds(h * H, H)
            eg = eb[rows, cols].astype(F32) * gain_ref[:, cols].astype(F32)
            g[h, rows, :] = (ga * eg + gb * mixed[h, rows, :]).astype(BF16)
        gall[rows, :] = g[c, rows, :]
        return 0

    lax.fori_loop(0, TOK // 64, gradient, 0)
    start(remote(g.at[1 - c], gall.at[pl.ds(TOK, TOK)], h_send.at[0], h_recv.at[0], sibling))
    stores = []
    for h in range(2):
        copy = pltpu.make_async_copy(g.at[h], rg_hbm.at[:, pl.ds(h * H, H)], loc.at[5 + h])
        copy.start()
        stores.append(copy)
    for n in range(4):
        theirs = ot.at[2 * n : 2 * n + 2, :, :, TOK : 2 * TOK]
        remote(theirs, theirs, o_send.at[n], o_recv.at[n], sibling).wait_recv()
    theirs = gall.at[pl.ds(TOK, TOK)]
    remote(theirs, theirs, h_send.at[0], h_recv.at[0], sibling).wait_recv()

    def slot(event):
        kind, d, k = event[:3]
        if kind == "Ay":
            n = (0 if d == "L" else 2) + k - 1
            return sa.at[n, event[3]], ra.at[n, event[3]]
        if kind == "Az":
            n = (0 if d == "L" else 4) + k - 1
            return sa2.at[n], ra2.at[n]
        if kind == "Bz":
            n = (0 if d == "L" else 4) + k - 1
            return sb.at[n, event[3]], rb.at[n, event[3]]
        n = (0 if d == "L" else 2) + k - 1
        return sb2.at[n], rb2.at[n]

    def push(axis, event, value):
        src, dst = slot(event)
        src[...] = value.astype(src.dtype)
        start(remote(src, dst, r_send.at[S_ID[event]], r_recv.at[S_ID[event]], peer[axis, event[1]]))

    for op in SCATTER:
        got = 0.0
        for event in op.waits:
            _, dst = slot(event)
            remote(dst, dst, r_send.at[S_ID[event]], r_recv.at[S_ID[event]], sibling).wait_recv()
            got = got + dst[...].astype(F32)
        kind = op.key[0] if isinstance(op.key, tuple) else op.key
        if kind == "CA":
            yy = yat(Y_LEAVE[op.key[1]])
            lhs = ot[:, yy].reshape(8 * RB, 2 * TOK)
            da[:, yy] = jnp.dot(lhs, gall[:, 0:Q], preferred_element_type=F32).reshape(8, RB, Q)
            for axis, event in op.sends:
                push(axis, event, da[zat(Z_LEAVE[event[3]]), yy])
        elif kind == "CB":
            zz = zat(Z_LEAVE[op.key[1]])
            lhs = ot[zz].reshape(4 * RB, 2 * TOK)
            db[zz] = jnp.dot(lhs, gall[:, Q:H], preferred_element_type=F32).reshape(4, RB, Q)
            for axis, event in op.sends:
                push(axis, event, db[zz, yat(Y_LEAVE[event[3]])])
        elif kind == "FA":
            push(*op.sends[0], da[zat(Z_LEAVE[op.key[1]]), yat(1)] + got)
        elif kind == "TA":
            value = da[zat(Z_LEAVE[op.key[1]]), y] + got
            if op.sends:
                push(*op.sends[0], value)
            else:
                fin[0:2] = value.reshape(2, RB // 2, Q)
        elif kind == "FB":
            value = db[zat(Z_LEAVE[op.key[1]]), yat(Y_LEAVE[op.key[2]])] + got
            if op.sends:
                push(*op.sends[0], value)
            else:
                fin[2:4] = value.reshape(2, RB // 2, Q)
        elif kind == "attn":
            n = op.key[1]
            cols = pl.ds(n * Q, Q)
            w0 = wbuf[0, 2 * n : 2 * n + 2].reshape(Q, H)
            w1 = wbuf[1, 2 * n : 2 * n + 2].reshape(Q, H)
            dims = (((1,), (1,)), ((), ()))
            acc = lax.dot_general(g[0], w0, dims, preferred_element_type=F32)
            acc = acc + lax.dot_general(g[1], w1, dims, preferred_element_type=F32)
            attn[:, cols] = acc.astype(BF16)
            copy = pltpu.make_async_copy(attn.at[:, cols], ag_hbm.at[:, cols], loc.at[7 + n])
            copy.start()
            stores.append(copy)
        else:
            square = jnp.zeros((8, 1), F32)
            for p in range(PPG):
                member = prow == gi * PPG + p
                base = jnp.sum(jnp.where(member, total, 0.0), axis=1, keepdims=True) * (1.0 / SAMPLES)
                off = jnp.where(member, total - base, 0.0)
                square = square + jnp.sum(off * off, axis=1, keepdims=True)
            lmsg1[...] = jnp.broadcast_to(square, (8, 128))
            start(remote(lmsg1, ls, l_send.at[0], l_recv.at[0], sibling))

    for k in range(3):
        start(remote(fin.at[xs[k]], xr.at[k], x_send.at[k], x_recv.at[k], dev(xs[k], c, z, y)))
    remote(ls, ls, l_send.at[0], l_recv.at[0], sibling).wait_recv()
    pair = lmsg1[...] + ls[...]
    lmsg2[...] = pair
    lx[x] = pair
    for k in range(3):
        start(remote(lmsg2, lx.at[x], m_send.at[k], m_recv.at[k], dev(xs[k], c, z, y)))
    value = fin[x]
    for k in range(3):
        remote(xr.at[k], xr.at[k], x_send.at[k], x_recv.at[k], sibling).wait_recv()
        value = value + xr[k]
    xg[c, x] = value * (1.0 / 512.0)
    for k in range(3):
        start(remote(xg.at[c, x], xg.at[c, x], w_send.at[k], w_recv.at[k], dev(xs[k], c, z, y)))
    start(remote(xg.at[c, x], xg.at[c, x], c_send.at[3], c_recv.at[3], sibling))
    for k in range(3):
        src = lax.rem(x + NX - 1 - k, NX)
        blk = xg.at[c, src]
        remote(blk, blk, w_send.at[k], w_recv.at[k], sibling).wait_recv()
        start(remote(blk, blk, c_send.at[k], c_recv.at[k], sibling))
    for k in range(3):
        src = lax.rem(x + NX - 1 - k, NX)
        remote(lx.at[src], lx.at[src], m_send.at[k], m_recv.at[k], sibling).wait_recv()
    whole = (lx[0] + lx[1]) + (lx[2] + lx[3])
    loss_ref[0, 0] = jnp.sum(whole[0:1, 0:1]) * (1.0 / (512 * SEQ))
    for k in range(4):
        src = x if k == 3 else lax.rem(x + NX - 1 - k, NX)
        blk = xg.at[1 - c, src]
        remote(blk, blk, c_send.at[k], c_recv.at[k], sibling).wait_recv()
    for h in range(2):
        for q in range(4):
            rows = pl.ds((q % 2) * 24, 24)
            cols = pl.ds(h * H + (q // 2) * Q, Q)
            wg_ref[rows, cols] = xg[h, q]
    for copy in stores:
        copy.wait()
    for copy in sent:
        copy.wait_send()


def local(
    resid_in, attn_out, target_rows, out_weight, norm_gain,
    seq_lengths, prompt_ids, log_offsets, plan_dest, plan_slot,
):
    hbm = pl.BlockSpec(memory_space=pl.ANY)
    vmem = pl.BlockSpec(memory_space=pltpu.VMEM)
    smem = pl.BlockSpec(memory_space=pltpu.SMEM)
    dma = pltpu.SemaphoreType.DMA
    n_g, n_s = len(G_ID), len(S_ID)
    scratch = [
        pltpu.VMEM((2, NZ, NY, RB, H), BF16),
        pltpu.VMEM((TOK, D), BF16),
        pltpu.VMEM((TOK, D), BF16),
        pltpu.VMEM((TOK, D), BF16),
        pltpu.VMEM((NZ, NY, RB, 2 * TOK), BF16),
        pltpu.VMEM((2, TOK, H), F32),
        pltpu.VMEM((TOK, 128), F32),
        pltpu.VMEM((TOK, 128), F32),
        pltpu.VMEM((2, TOK, H), BF16),
        pltpu.VMEM((2 * TOK, H), BF16),
        pltpu.VMEM((TOK, D), BF16),
        pltpu.VMEM((NZ, NY, RB, Q), F32),
        pltpu.VMEM((NZ, NY, RB, Q), F32),
        pltpu.VMEM((3, 8, RB, Q), BF16),
        pltpu.VMEM((3, 8, RB, Q), BF16),
        pltpu.VMEM((7, RB, Q), F32),
        pltpu.VMEM((7, RB, Q), F32),
        pltpu.VMEM((7, 4, RB, Q), BF16),
        pltpu.VMEM((7, 4, RB, Q), BF16),
        pltpu.VMEM((3, RB, Q), F32),
        pltpu.VMEM((3, RB, Q), F32),
        pltpu.VMEM((4, RB // 2, Q), F32),
        pltpu.VMEM((3, RB // 2, Q), F32),
        pltpu.VMEM((2, 4, RB // 2, Q), F32),
        pltpu.VMEM((RB // 2, Q), F32),
        pltpu.VMEM((3, 8, 128), F32),
        pltpu.VMEM((7, 8, 128), F32),
        pltpu.VMEM((8, 128), F32),
        pltpu.VMEM((8, 128), F32),
        pltpu.VMEM((8, 128), F32),
        pltpu.VMEM((4, 8, 128), F32),
        pltpu.VMEM((8, 128), F32),
        pltpu.VMEM((8, 128), F32),
        pltpu.VMEM((2, 8, 128), F32),
        dma((11,)),
        dma((n_g,)), dma((n_g,)), dma((n_g,)), dma((n_g,)),
        dma((4,)), dma((4,)), dma((1,)), dma((1,)),
        dma((n_s,)), dma((n_s,)),
        dma((3,)), dma((3,)), dma((7,)), dma((7,)),
        dma((3,)), dma((3,)), dma((3,)), dma((3,)), dma((4,)), dma((4,)),
        dma((1,)), dma((1,)), dma((3,)), dma((3,)),
    ]
    call = pl.pallas_call(
        kernel,
        out_shape=(
            jax.ShapeDtypeStruct((TOK, D), BF16),
            jax.ShapeDtypeStruct((TOK, D), BF16),
            jax.ShapeDtypeStruct((RB, D), F32),
            jax.ShapeDtypeStruct((1, 1), F32),
        ),
        in_specs=[hbm, hbm, hbm, hbm, vmem, smem, smem, smem, vmem],
        out_specs=(hbm, hbm, vmem, smem),
        scratch_shapes=scratch,
        name="balance",
        compiler_params=pltpu.CompilerParams(
            collective_id=0, has_side_effects=True, vmem_limit_bytes=60 * 1024 * 1024
        ),
        cost_estimate=pl.CostEstimate(flops=9060000000, bytes_accessed=10000000, transcendentals=640),
    )
    rg, ag, wg, loss = call(
        resid_in.reshape(TOK, D),
        attn_out.reshape(TOK, D),
        target_rows.reshape(TOK, D),
        out_weight,
        norm_gain.reshape(1, D),
        seq_lengths,
        prompt_ids,
        log_offsets,
        prompt_ids.reshape(4, 128),
    )
    return rg.reshape(2, SEQ, D), ag.reshape(2, SEQ, D), wg, loss.reshape(())


def solution(mesh):
    return jax.shard_map(
        local,
        mesh=mesh,
        in_specs=(
            P(("group", "fsdp"), None, None),
            P(("group", "fsdp"), None, None),
            P(("group", "fsdp"), None, None),
            P("fsdp", None),
            P(), P(), P(), P(), P(), P(),
        ),
        out_specs=(
            P(("group", "fsdp"), None, None),
            P(("group", "fsdp"), None, None),
            P("fsdp", None),
            P(),
        ),
        check_vma=False,
    )
```

time: 528 us -> 104 us (0.20)
  waiting for transfers between devices: 328 us -> 0 us
  blocking collectives: 136 us -> 0 us
  Pallas kernels: 0 us -> 94.7 us
  matrix products: 20.2 us -> 0 us
  between operations: 15.6 us -> 2.46 us
  local copies, waits for them, and re-layouts: 18.2 us -> 6.36 us
  other arithmetic: 9.56 us -> 0 us
    unnamed x4 -> x0, waiting for transfers between devices: 243 us -> none
    psum x2 -> x0, blocking collectives: 136 us -> none  [the longest x1 78.9 us: local(): square_total = lax.psum(jnp.sum(centred * centred), ('group', 'fsdp'))]
    pallas_call x0 -> x1, Pallas kernels: none -> 94.7 us  [local(): call(resid_in.reshape(TOK, D), attn_out.reshape(TOK, D), target_rows.resh...]
    all_gather x1 -> x0, waiting for transfers between devices: 85.1 us -> none  [local(): weight = lax.all_gather(out_weight, 'fsdp', axis=0, tiled=True)]
    dot_general x3 -> x0, matrix products: 20.2 us -> none  [the longest x1 7.45 us: backward_rows(): lax.dot_general(grad_rows, weight, (((1,), (1,)), ((), ())), preferred_el...]
    unnamed x15 -> x7, local copies, waits for them, and re-layouts: 16.5 us -> 5.08 us
    reduce_sum x6 -> x0, other arithmetic: 5.62 us -> none  [the longest x1 3.78 us: backward_rows(): inner = jnp.mean(mixed * gained, axis=-1, keepdims=True)]
  transfers between devices with their start and end apart: 3 -> 0, of which waited for: 2 -> 0; matrix products, arithmetic and copies ran while one was open for 2% -> 0% of each run, Pallas kernels for 0% -> 0%
where the time goes in v1:
time: 104 us; the launch traced here: 103 us
  Pallas kernels  94.7 us (91%)
  local copies, waits for them, and re-layouts  6.36 us (6%)
  between operations  2.46 us (2%)
    pallas_call x1, Pallas kernels, local(): call(resid_in.reshape(TOK, D), attn_out.reshape(TOK, D), target_rows.resh...  94.7 us
    unnamed x7, local copies, waits for them, and re-layouts  5.08 us

profile of v1, /device:TPU:1, one launch (start us, length us, event | category | flops | bytes accessed | tf_op | source)
XLA Modules:
  0.0 103.5 jit_solution(7654419039464544043)
XLA Ops:
  0.6 1.3 %reshape.35.gain_ref = bf16[1,1536]{1,0:T(2,128)(2,1)} reshape(bf16[1536]{0:T(1024)(128)(2,1)} %param.14) | data formatting | bytes 6144 | tf_op jit(solution)/shard_map/reshape | solution.py:537
  1.9 94.7 %balance.1 = (bf16[640,1536]{1,0:T(8,128)(2,1)}, bf16[640,1536]{1,0:T(8,128)(2,1)}, f32[48,1536]{1,0:T(8,128)}, f32[1,1]{1,0:T(1,128)}) custom-call(bf16[640,1536]{1,0:T(8,128)(2,1)} %bitcast.9, bf16[640,1536]{1,0:T(8,128)(2,1)} %bitcast.10, bf16[640,1536]{1,0:T(8,128)(2,1)} %bitcast.11, bf16[48,1536]{1,0:T(8,128)(2,1)} %w_hbm.1, ...), custom_call_target="tpu_custom_call" | custom-call | flops 9059999744 | bytes 10000000 | tf_op jit(solution)/shard_map/balance/pallas_call | solution.py:532
  96.6 0.0 copy-start
  96.6 3.1 %copy.16 = bf16[2,320,1536]{2,1,0:T(8,128)(2,1)} copy(bf16[2,320,1536]{2,1,0:T(8,128)(2,1)} %bitcast.8) | data formatting | bytes 3932160
  99.7 0.0 copy-done
  99.7 0.0 copy-start.1
  99.7 1.3 %copy.17 = bf16[2,320,1536]{2,1,0:T(8,128)(2,1)} copy(bf16[2,320,1536]{2,1,0:T(8,128)(2,1)S(1)} %bitcast.7) | data formatting | bytes 3932160
  101.0 0.0 copy-done.1
  101.0 0.7 copy.18
Async XLA Ops:
  96.6 3.1 %copy-start = (bf16[640,1536]{1,0:T(8,128)(2,1)S(1)}, bf16[640,1536]{1,0:T(8,128)(2,1)}, u32[]{:S(2)}) copy-start(bf16[640,1536]{1,0:T(8,128)(2,1)} %get-tuple-element.9) | copy-start | bytes 5898244
  99.7 1.3 %copy-start.1 = (f32[48,1536]{1,0:T(8,128)S(1)}, f32[48,1536]{1,0:T(8,128)}, u32[]{:S(2)}) copy-start(f32[48,1536]{1,0:T(8,128)} %get-tuple-element.18) | copy-start | bytes 884740

commit v2 on v1

v2 whole, which is shorter than its diff:
```python
import functools
import math

import jax
import jax.numpy as jnp
from jax import lax
from jax.experimental import pallas as pl
from jax.experimental.pallas import tpu as pltpu
from jax.sharding import PartitionSpec as P

MESH = pl.DeviceIdType.MESH
F32, BF16 = jnp.float32, jnp.bfloat16
NX, NC, NZ, NY = 4, 2, 8, 4
EPS = 1e-06
PPG = 8
SAMPLES = 8
D = 1536
TOK = 640
SEQ = 320
H = D // 2
Q = D // 4
RB = 48

Z_ARRIVE = (0, -1, 1, -2, 2, -3, 3, -4)
Y_ARRIVE = (0, -1, 1, -2)
Z_LEAVE = (4, -3, 3, -2, 2, -1, 1, 0)
Y_LEAVE = (2, -1, 1, 0)


class Op:
    def __init__(self, key, waits=(), after=(), sends=(), cost=0.1, rank=0):
        self.key, self.waits, self.after, self.sends, self.cost, self.rank = key, waits, after, sends, cost, rank


def order(ops, size):
    now, done, at, free, out = 0.0, set(), {}, {}, []
    left = list(ops)
    while left:
        best = None
        for n, op in enumerate(left):
            if all(a in done for a in op.after) and all(w in at for w in op.waits):
                ready = max([now] + [at[w] for w in op.waits])
                score = (ready, op.rank, n)
                if best is None or score < best[0]:
                    best = (score, op)
        (ready, _, _), op = best
        left.remove(op)
        now = ready + op.cost
        for axis, event in op.sends:
            free[axis] = max(now, free.get(axis, 0.0)) + size(event)
            at[event] = free[axis] + (0.9 if axis == "s" else 2.0 if size(event) > 0.5 else 1.6)
        done.add(op.key)
        out.append(op)
    return out


def hops(event):
    return abs(TO[event[0], event[1]]) if event[0] in ("Az", "By") else 2 if event[1] == "D" else 1


GATHER_TO = {-1: 1, 1: -1, -2: 2, 2: -2, -3: 1, 3: -1, -4: 2}
SCATTER_TO = {4: 2, 3: 1, -3: -1, -2: -2, 2: 2, -1: -1, 1: 1}
TO = {}


def gather_ops():
    ops = []
    TO.clear()
    TO.update({("Az", n): v for n, v in GATHER_TO.items()})
    TO.update({("By", n): GATHER_TO[n] for n in (-1, 1, -2)})

    def a_first(off):
        sends = [("y", ("Ay", "L", 1, off)), ("y", ("Ay", "S", 1, off))]
        if off in LATE:
            sends.append(("y", ("Ay", "D", 2, off)))
        if off == 0:
            sends = [("z", ("Az", n)) for n in (-2, 2, -1, 1)] + sends
        if off == -2:
            sends = [("z", ("Az", -4)), ("z", ("Az", -3))] + sends
        if off == 2:
            sends = [("z", ("Az", 3))] + sends
        return sends

    def b_first(off):
        sends = [("z", ("Bz", "L", 1, off)), ("z", ("Bz", "S", 1, off))]
        if off == 0:
            sends = [("y", ("By", n)) for n in (-2, -1, 1)] + sends
        return sends

    ops.append(Op("start", sends=a_first(0)[:4] + b_first(0) + a_first(0)[4:]))
    for off in Z_ARRIVE[1:]:
        ops.append(Op(("Az", off), waits=[("Az", off)], after=["start"], sends=a_first(off)))
    for off in Y_ARRIVE[1:]:
        ops.append(Op(("By", off), waits=[("By", off)], after=["start"], sends=b_first(off)))
    for off in Z_ARRIVE:
        for d, k in (("L", 1), ("D", 2) if off in LATE else ("L", 2), ("S", 1)):
            event = ("Ay", d, k, off)
            sends = [("y", ("Ay", d, k + 1, off))] if k == 1 and d == "L" and off not in LATE else []
            ops.append(Op(event, waits=[event], after=["start"], sends=sends))
    for off in Y_ARRIVE:
        for d, last in (("L", 4), ("S", 3)):
            for k in range(1, last + 1):
                event = ("Bz", d, k, off)
                sends = [("z", ("Bz", d, k + 1, off))] if k < last else []
                ops.append(Op(event, waits=[event], after=["start"], sends=sends))
    return ops


LATE = (-3, 3, -4)


def scatter_ops():
    ops = []
    TO.clear()
    TO.update({("Az", n): v for n, v in SCATTER_TO.items()})
    TO.update({("By", n): SCATTER_TO[n] for n in (2, -1, 1)})
    for n, yo in enumerate(Y_LEAVE):
        sends = []
        if n == 0:
            sends = [("y", ("Ay", "L", 1, i)) for i in range(8)]
        if n == 1:
            sends = [("y", ("Ay", "S", 1, i)) for i in range(8)]
        ops.append(Op(("CA", n), sends=sends, cost=0.6, rank=2 + n))
    for i, zo in enumerate(Z_LEAVE):
        sends = []
        if i == 0:
            sends = [("z", ("Bz", "L", 1, j)) for j in range(4)]
        if i == 1:
            sends = [("z", ("Bz", "S", 1, j)) for j in range(4)]
        ops.append(Op(("CB", i), sends=sends, cost=0.35, rank=2 + i / 2))
    for i, off in enumerate(Z_LEAVE):
        ops.append(Op(("FA", i), waits=[("Ay", "L", 1, i)], after=[("CA", 0), ("CA", 2)], sends=[("y", ("Ay", "L", 2, i))]))
        waits = [("Ay", "L", 2, i), ("Ay", "S", 1, i)]
        waits += [("Az", n) for n in {2: (4, 3), -2: (-3,), 0: (2, -2, 1, -1)}.get(off, ())]
        sends = [("z", ("Az", off))] if off else [("x", ("X", 0, k)) for k in range(3)]
        ops.append(Op(("TA", i), waits=waits, after=[("CA", 3)], sends=sends))
    for i in range(2, 8):
        for j, off in enumerate(Y_LEAVE):
            if i < 7:
                waits = [("Bz", "LS"[i % 2], i // 2, j)]
                sends = [("z", ("Bz", "LS"[i % 2], i // 2 + 1, j))]
            else:
                waits = [("Bz", "L", 4, j), ("Bz", "S", 3, j)]
                sends = [("y", ("By", off))]
                if off == 0:
                    waits += [("By", 2), ("By", -1), ("By", 1)]
                    sends = [("x", ("X", 1, k)) for k in range(3)]
            ops.append(Op(("FB", i, j), waits=waits, after=[("CB", i)], sends=sends))
    for ab in range(2):
        ops.append(Op(("X", ab), waits=[("X", ab, k) for k in range(3)], sends=[("s", ("G", ab))]))
    for ab in range(2):
        ops.append(Op(("W", ab), waits=[("G", ab)]))
    ops.append(Op("loss", after=[("CA", 3), ("CB", 7)], cost=1.0, rank=20, sends=[("s", ("l1",))]))
    ops.append(Op("pair", waits=[("l1",)], sends=[("x", ("l2", k)) for k in range(3)]))
    ops.append(Op("total", waits=[("l2", k) for k in range(3)]))
    for n in range(4):
        ops.append(Op(("attn", n), after=[("CA", 3), ("CB", 7)], cost=1.2, rank=30 + n))
    return ops


def size(event):
    if event[0] in ("l1", "l2"):
        return 0.05
    if event[0] == "X":
        return 1.1
    if event[0] == "G":
        return 0.15
    return 0.4 * hops(event)


GATHER = order(gather_ops(), size)
SCATTER = order(scatter_ops(), size)
G_ID = {e: n for n, e in enumerate(e for op in GATHER for _, e in op.sends)}
S_ID = {e: n for n, e in enumerate(e for op in SCATTER for _, e in op.sends)}


def kernel(
    x_hbm, o_hbm, e_hbm, w_hbm, gain_hbm, len_hbm, pid_hbm, off_hbm, prow_hbm,
    rg_out, ag_out, wg_ref, loss_ref,
    wbuf, xb, ob, eb, ot, mixed, ss_ref, t_ref, g, gall,
    da, db, sa, ra, sa2, ra2, sb, rb, sb2, rb2,
    xr, xg, my, mz, msg1, msg2, ls, lx, lmsg1, lmsg2, crow,
    gain_in, gain_ref, len_ref, pid_ref, off_ref, prow_ref, gauge,
    loc, g_send, g_recv, b_send, b_recv, o_send, o_recv, h_send, h_recv, r_recv,
    a_send, a2_send, s_send, s2_send, x_send, q_send, y_send, y_recv, z_send, z_recv, l_send, m_send,
):
    gi, fi = lax.axis_index("group"), lax.axis_index("fsdp")
    x, c = gi // 2, lax.rem(gi, 2)
    z, y = fi // 4, lax.rem(fi, 4)
    s = 1 - 2 * c

    z_off = {off: lax.rem(z + off * s + 2 * NZ, NZ) for off in range(-4, 5)}
    y_off = {off: lax.rem(y + off * s + 2 * NY, NY) for off in range(-2, 3)}
    zat, yat = z_off.get, y_off.get

    def dev(xx, cc, zz, yy):
        return (xx * 2 + cc, zz * 4 + yy)

    def peer(event, to):
        kind, d = event[:2]
        if kind in ("Az", "By"):
            return dev(x, c, zat(to[d]), y) if kind == "Az" else dev(x, c, z, yat(to[d]))
        step = {"L": 1, "S": -1, "D": 2}[d]
        return dev(x, c, zat(step), y) if kind == "Bz" else dev(x, c, z, yat(step))

    sibling = dev(x, 1 - c, z, y)
    xs = [lax.rem(x + k, NX) for k in range(1, NX)]
    ys = [lax.rem(y + k, NY) for k in range(1, NY)]
    zs = [lax.rem(z + k, NZ) for k in range(1, NZ)]

    def remote(src, dst, send, recv, to):
        return pltpu.make_async_remote_copy(
            src_ref=src, dst_ref=dst, send_sem=send, recv_sem=recv, device_id=to, device_id_type=MESH
        )

    sent = []

    def start(copy):
        copy.start()
        sent.append(copy)

    loads = [
        pltpu.make_async_copy(w_hbm.at[:, 0:H], wbuf.at[0, z, y], loc.at[0]),
        pltpu.make_async_copy(w_hbm.at[:, H:D], wbuf.at[1, z, y], loc.at[1]),
        pltpu.make_async_copy(o_hbm, ob, loc.at[2]),
        pltpu.make_async_copy(x_hbm, xb, loc.at[3]),
        pltpu.make_async_copy(e_hbm, eb, loc.at[4]),
        pltpu.make_async_copy(gain_hbm, gain_in, loc.at[5]),
        pltpu.make_async_copy(len_hbm, len_ref, loc.at[6]),
        pltpu.make_async_copy(pid_hbm, pid_ref, loc.at[7]),
        pltpu.make_async_copy(off_hbm, off_ref, loc.at[8]),
        pltpu.make_async_copy(prow_hbm, prow_ref, loc.at[9]),
    ]
    for copy in loads:
        copy.start()

    barrier = pltpu.get_barrier_semaphore()
    greet = [sibling]
    greet += [dev(v, c, z, y) for v in xs] + [dev(x, c, z, v) for v in ys] + [dev(x, c, v, y) for v in zs]
    for to in greet:
        pl.semaphore_signal(barrier, inc=1, device_id=to, device_id_type=MESH)
    pl.semaphore_wait(barrier, len(greet))

    loads[0].wait()
    loads[1].wait()

    def block_of(event, sender):
        kind = event[0]
        if kind in ("Az", "By"):
            step = event[1]
            if sender:
                step += GATHER_TO[step]
            zz, yy = (zat(step), y) if kind == "Az" else (z, yat(step))
        else:
            d, k, off = event[1:]
            k = (0 if d == "D" else k - 1) if sender else k
            step = k if d == "S" else -k
            zz, yy = (zat(off), yat(step)) if kind == "Ay" else (zat(step), yat(off))
        cols = pl.ds(0, Q) if kind[0] == "A" else pl.ds(Q, Q)
        return wbuf.at[c, zz, yy, :, cols]

    def turn(n):
        piece = ob[:, pl.ds(n * Q, Q)].T
        ot[2 * n : 2 * n + 2, :, :, 0:TOK] = piece.reshape(2, 4, RB, TOK)
        part = ot.at[2 * n : 2 * n + 2, :, :, 0:TOK]
        start(remote(part, ot.at[2 * n : 2 * n + 2, :, :, TOK : 2 * TOK], o_send.at[n], o_recv.at[n], sibling))

    turn_at = {4: 0, 10: 1, 18: 2, 26: 3}
    for step, op in enumerate(GATHER):
        for event in op.waits:
            mine = block_of(event, False)
            remote(mine, mine, g_send.at[0], g_recv.at[G_ID[event]], sibling).wait_recv()
        for axis, event in op.sends:
            part = 0 if event[0][0] == "A" else 1
            blk = block_of(event, True)
            remote(blk, blk, g_send.at[part], g_recv.at[G_ID[event]], peer(event, GATHER_TO)).start()
        for event in op.waits:
            part = 0 if event[0][0] == "A" else 1
            mine = block_of(event, False)
            remote(mine, mine, b_send.at[part], b_recv.at[part], sibling).start()
        if step == 0:
            loads[2].wait()
        if step in turn_at:
            turn(turn_at[step])
    for part in range(2):
        remote(gauge, gauge, b_send.at[part], b_recv.at[part], sibling).wait_recv()
    for copy in loads[3:]:
        copy.wait()
    wide = gain_in[...].astype(F32)
    gain_ref[...] = jnp.concatenate([wide[n : n + 1] for n in range(D // 128)], axis=1)

    def forward(m, _):
        rows = pl.ds(pl.multiple_of(m * 160, 160), 160)
        ss = jnp.zeros((160, 1), F32)
        tt = jnp.zeros((160, 1), F32)
        for h in range(2):
            cols = pl.ds(h * H, H)
            w = wbuf[h].reshape(D, H)
            acc = jnp.dot(ob[rows, :], w, preferred_element_type=F32) + xb[rows, cols].astype(F32)
            mixed[h, rows, :] = acc
            eg = eb[rows, cols].astype(F32) * gain_ref[:, cols]
            ss = ss + jnp.sum(acc * acc, axis=1, keepdims=True)
            tt = tt + jnp.sum(acc * eg, axis=1, keepdims=True)
        ss_ref[rows, :] = jnp.broadcast_to(ss, (160, 128))
        t_ref[rows, :] = jnp.broadcast_to(tt, (160, 128))
        return 0

    lax.fori_loop(0, TOK // 160, forward, 0)

    first = (gi * 32 + fi) * 2
    lane = lax.broadcasted_iota(jnp.int32, (8, 128), 1)
    pos = lax.broadcasted_iota(jnp.int32, (SEQ, 128), 0)
    root = 1.0 / math.sqrt(D)
    deltas = []
    for j in range(2):
        rows = pl.ds(j * SEQ, SEQ)
        mask = (pos < len_ref[first + j]).astype(F32)
        scale = lax.rsqrt(ss_ref[rows, :] * (1.0 / D) + EPS)
        t = t_ref[rows, :]
        logp = t * scale * mask * root
        deltas.append(jnp.broadcast_to(jnp.sum(logp, axis=0, keepdims=True), (8, 128)) + off_ref[first + j])
        ss_ref[rows, :] = scale * mask * root
        t_ref[rows, :] = -(scale * scale * scale) * mask * (t * (root / D))
    at = lax.rem(gi, 2) * 64 + 2 * fi
    msg1[...] = jnp.where(lane == at, deltas[0], jnp.where(lane == at + 1, deltas[1], 0.0))

    def prepare(m, _):
        rows = pl.ds(pl.multiple_of(m * 64, 64), 64)
        ga = jnp.concatenate([ss_ref[rows, :]] * 6, axis=1)
        gb = jnp.concatenate([t_ref[rows, :]] * 6, axis=1)
        for h in range(2):
            cols = pl.ds(h * H, H)
            eg = eb[rows, cols].astype(F32) * gain_ref[:, cols]
            mixed[h, rows, :] = ga * eg + gb * mixed[h, rows, :]
        return 0

    for k in range(3):
        start(remote(msg1, my.at[k], y_send.at[k], y_recv.at[k], dev(x, c, z, ys[k])))
    lax.fori_loop(0, 4, prepare, 0)
    total = msg1[...]
    for k in range(3):
        remote(my.at[k], my.at[k], y_send.at[k], y_recv.at[k], sibling).wait_recv()
        total = total + my[k]
    msg2[...] = total
    for k in range(7):
        start(remote(msg2, mz.at[k], z_send.at[k], z_recv.at[k], dev(x, c, zs[k], y)))
    lax.fori_loop(4, 10, prepare, 0)
    for part in range(2):
        remote(gauge, gauge, g_send.at[part], g_recv.at[0], sibling).wait_send()
        remote(gauge, gauge, b_send.at[part], g_recv.at[0], sibling).wait_send()
    for k in range(7):
        remote(mz.at[k], mz.at[k], z_send.at[k], z_recv.at[k], sibling).wait_recv()
        total = total + mz[k]

    prow = jnp.broadcast_to(prow_ref[pl.ds(gi // 2, 1), :], (8, 128))
    for j in range(2):
        base = jnp.sum(jnp.where(prow == pid_ref[first + j], total, 0.0), axis=1, keepdims=True) * (1.0 / SAMPLES)
        crow[j] = deltas[j] - base

    def gradient(m, _):
        rows = pl.ds(pl.multiple_of(m * 64, 64), 64)
        cc = jnp.where(m < 5, crow[0], crow[1])[0:1]
        cc = jnp.concatenate([cc] * 6, axis=1)
        for h in range(2):
            value = (mixed[h, rows, :] * cc).astype(BF16)
            g[h, rows, :] = value
            rg_out[rows, h * H : (h + 1) * H] = value
        gall[rows, :] = g[c, rows, :]
        return 0

    lax.fori_loop(0, TOK // 64, gradient, 0)
    start(remote(g.at[1 - c], gall.at[pl.ds(TOK, TOK)], h_send.at[0], h_recv.at[0], sibling))
    for n in range(4):
        theirs = ot.at[2 * n : 2 * n + 2, :, :, TOK : 2 * TOK]
        remote(theirs, theirs, o_send.at[n], o_recv.at[n], sibling).wait_recv()
    theirs = gall.at[pl.ds(TOK, TOK)]
    remote(theirs, theirs, h_send.at[0], h_recv.at[0], sibling).wait_recv()

    def slot(event):
        kind, d = event[:2]
        if kind == "Ay":
            n = (0 if d == "L" else 2) + event[2] - 1
            return sa.at[n, event[3]], ra.at[n, event[3]], a_send
        if kind == "Az":
            n = list(SCATTER_TO).index(d)
            return sa2.at[n], ra2.at[n], a2_send
        if kind == "Bz":
            n = (0 if d == "L" else 4) + event[2] - 1
            return sb.at[n, event[3]], rb.at[n, event[3]], s_send
        n = (2, -1, 1).index(d)
        return sb2.at[n], rb2.at[n], s2_send

    def push(event, value):
        src, dst, sem = slot(event)
        src[...] = value.astype(BF16)
        remote(src, dst, sem.at[0], r_recv.at[S_ID[event]], peer(event, SCATTER_TO)).start()

    def got_of(event):
        if event[0] == "X":
            return xr.at[event[1], lax.rem(x + NX - 1 - event[2], NX)]
        if event[0] == "G":
            return xg.at[1 - c, event[1]]
        if event[0] == "l1":
            return ls
        if event[0] == "l2":
            return lx.at[lax.rem(x + NX - 1 - event[1], NX)]
        return slot(event)[1]

    def spread(ab, value):
        xr[ab, x] = value
        for k in range(3):
            blk = xr.at[ab, x]
            remote(blk, blk, x_send.at[ab], r_recv.at[S_ID["X", ab, k]], dev(xs[k], c, z, y)).start()

    for op in SCATTER:
        got = 0.0
        for event in op.waits:
            dst = got_of(event)
            remote(dst, dst, a_send.at[0], r_recv.at[S_ID[event]], sibling).wait_recv()
            if event[0] in ("Ay", "Az", "By", "Bz"):
                got = got + dst[...].astype(F32)
        kind = op.key[0] if isinstance(op.key, tuple) else op.key
        if kind == "CA":
            yy = yat(Y_LEAVE[op.key[1]])
            lhs = ot[:, yy].reshape(8 * RB, 2 * TOK)
            da[:, yy] = jnp.dot(lhs, gall[:, 0:Q], preferred_element_type=F32).reshape(8, RB, Q)
            for axis, event in op.sends:
                push(event, da[zat(Z_LEAVE[event[3]]), yy])
        elif kind == "CB":
            zz = zat(Z_LEAVE[op.key[1]])
            lhs = ot[zz].reshape(4 * RB, 2 * TOK)
            db[zz] = jnp.dot(lhs, gall[:, Q:H], preferred_element_type=F32).reshape(4, RB, Q)
            for axis, event in op.sends:
                push(event, db[zz, yat(Y_LEAVE[event[3]])])
        elif kind == "FA":
            push(op.sends[0][1], da[zat(Z_LEAVE[op.key[1]]), yat(1)] + got)
        elif kind == "TA":
            value = da[zat(Z_LEAVE[op.key[1]]), y] + got
            if Z_LEAVE[op.key[1]]:
                push(op.sends[0][1], value)
            else:
                spread(0, value)
        elif kind == "FB":
            value = db[zat(Z_LEAVE[op.key[1]]), yat(Y_LEAVE[op.key[2]])] + got
            if op.sends[0][0] != "x":
                push(op.sends[0][1], value)
            else:
                spread(1, value)
        elif kind == "X":
            ab = op.key[1]
            value = ((xr[ab, 0] + xr[ab, 1]) + (xr[ab, 2] + xr[ab, 3])) * (1.0 / 512.0)
            xg[c, ab] = value
            blk = xg.at[c, ab]
            start(remote(blk, blk, q_send.at[ab], r_recv.at[S_ID["G", ab]], sibling))
        elif kind == "W":
            ab = op.key[1]
            for h in range(2):
                wg_ref[:, pl.ds(h * H + ab * Q, Q)] = xg[h, ab]
        elif kind == "pair":
            pair = lmsg1[...] + ls[...]
            lmsg2[...] = pair
            lx[x] = pair
            for k in range(3):
                start(remote(lmsg2, lx.at[x], m_send.at[k], r_recv.at[S_ID["l2", k]], dev(xs[k], c, z, y)))
        elif kind == "total":
            whole = (lx[0] + lx[1]) + (lx[2] + lx[3])
            loss_ref[0, 0] = jnp.sum(whole[0:1, 0:1]) * (1.0 / (512 * SEQ))
        elif kind == "attn":
            n = op.key[1]
            cols = pl.ds(n * Q, Q)
            w0 = wbuf[0, 2 * n : 2 * n + 2].reshape(Q, H)
            w1 = wbuf[1, 2 * n : 2 * n + 2].reshape(Q, H)
            dims = (((1,), (1,)), ((), ()))
            acc = lax.dot_general(g[0], w0, dims, preferred_element_type=F32)
            acc = acc + lax.dot_general(g[1], w1, dims, preferred_element_type=F32)
            ag_out[:, cols] = acc.astype(BF16)
        else:
            square = jnp.zeros((8, 1), F32)
            for p in range(PPG):
                member = prow == gi * PPG + p
                base = jnp.sum(jnp.where(member, total, 0.0), axis=1, keepdims=True) * (1.0 / SAMPLES)
                off = jnp.where(member, total - base, 0.0)
                square = square + jnp.sum(off * off, axis=1, keepdims=True)
            lmsg1[...] = jnp.broadcast_to(square, (8, 128))
            start(remote(lmsg1, ls, l_send.at[0], r_recv.at[S_ID[("l1",)]], sibling))

    for ref, sem in ((sa, a_send), (sa2, a2_send), (sb, s_send), (sb2, s2_send)):
        remote(ref, ref, sem.at[0], r_recv.at[0], sibling).wait_send()
    for ab in range(2):
        ref = xr.at[ab, 0:3]
        remote(ref, ref, x_send.at[ab], r_recv.at[0], sibling).wait_send()
    for copy in sent:
        copy.wait_send()


def local(
    resid_in, attn_out, target_rows, out_weight, norm_gain,
    seq_lengths, prompt_ids, log_offsets, plan_dest, plan_slot,
):
    hbm = pl.BlockSpec(memory_space=pl.ANY)
    vmem = pl.BlockSpec(memory_space=pltpu.VMEM)
    smem = pl.BlockSpec(memory_space=pltpu.SMEM)
    dma = pltpu.SemaphoreType.DMA
    n_g, n_s = len(G_ID), len(S_ID)
    scratch = [
        pltpu.VMEM((2, NZ, NY, RB, H), BF16),
        pltpu.VMEM((TOK, D), BF16),
        pltpu.VMEM((TOK, D), BF16),
        pltpu.VMEM((TOK, D), BF16),
        pltpu.VMEM((NZ, NY, RB, 2 * TOK), BF16),
        pltpu.VMEM((2, TOK, H), F32),
        pltpu.VMEM((TOK, 128), F32),
        pltpu.VMEM((TOK, 128), F32),
        pltpu.VMEM((2, TOK, H), BF16),
        pltpu.VMEM((2 * TOK, H), BF16),
        pltpu.VMEM((NZ, NY, RB, Q), F32),
        pltpu.VMEM((NZ, NY, RB, Q), F32),
        pltpu.VMEM((3, 8, RB, Q), BF16),
        pltpu.VMEM((3, 8, RB, Q), BF16),
        pltpu.VMEM((7, RB, Q), BF16),
        pltpu.VMEM((7, RB, Q), BF16),
        pltpu.VMEM((7, 4, RB, Q), BF16),
        pltpu.VMEM((7, 4, RB, Q), BF16),
        pltpu.VMEM((3, RB, Q), BF16),
        pltpu.VMEM((3, RB, Q), BF16),
        pltpu.VMEM((2, 4, RB, Q), F32),
        pltpu.VMEM((2, 2, RB, Q), F32),
        pltpu.VMEM((3, 8, 128), F32),
        pltpu.VMEM((7, 8, 128), F32),
        pltpu.VMEM((8, 128), F32),
        pltpu.VMEM((8, 128), F32),
        pltpu.VMEM((8, 128), F32),
        pltpu.VMEM((4, 8, 128), F32),
        pltpu.VMEM((8, 128), F32),
        pltpu.VMEM((8, 128), F32),
        pltpu.VMEM((2, 8, 128), F32),
        pltpu.VMEM((D // 128, 128), BF16),
        pltpu.VMEM((1, D), F32),
        pltpu.SMEM((512,), jnp.int32),
        pltpu.SMEM((512,), jnp.int32),
        pltpu.SMEM((512,), F32),
        pltpu.VMEM((4, 128), jnp.int32),
        pltpu.VMEM((31, RB, Q), BF16),
        dma((10,)),
        dma((2,)), dma((n_g,)), dma((2,)), dma((2,)),
        dma((4,)), dma((4,)), dma((1,)), dma((1,)),
        dma((n_s,)),
        dma((1,)), dma((1,)), dma((1,)), dma((1,)), dma((2,)), dma((2,)),
        dma((3,)), dma((3,)), dma((7,)), dma((7,)),
        dma((1,)), dma((3,)),
    ]
    call = pl.pallas_call(
        kernel,
        out_shape=(
            pltpu.VMEM((TOK, D), BF16),
            pltpu.VMEM((TOK, D), BF16),
            pltpu.VMEM((RB, D), F32),
            jax.ShapeDtypeStruct((1, 1), F32),
        ),
        in_specs=[hbm] * 9,
        out_specs=(vmem, vmem, vmem, smem),
        scratch_shapes=scratch,
        name="balance",
        compiler_params=pltpu.CompilerParams(
            collective_id=0, has_side_effects=True, vmem_limit_bytes=48 * 1024 * 1024
        ),
        cost_estimate=pl.CostEstimate(flops=9060000000, bytes_accessed=10000000, transcendentals=640),
    )
    operands = (
        resid_in.reshape(TOK, D),
        attn_out.reshape(TOK, D),
        target_rows.reshape(TOK, D),
        out_weight,
        norm_gain.reshape(D // 128, 128),
        seq_lengths,
        prompt_ids,
        log_offsets,
        prompt_ids.reshape(4, 128),
    )
    rg, ag, wg, loss = call(*(pltpu.with_memory_space_constraint(v, pltpu.HBM) for v in operands))
    return rg.reshape(2, SEQ, D), ag.reshape(2, SEQ, D), wg, loss.reshape(())


def solution(mesh):
    return jax.shard_map(
        local,
        mesh=mesh,
        in_specs=(
            P(("group", "fsdp"), None, None),
            P(("group", "fsdp"), None, None),
            P(("group", "fsdp"), None, None),
            P("fsdp", None),
            P(), P(), P(), P(), P(), P(),
        ),
        out_specs=(
            P(("group", "fsdp"), None, None),
            P(("group", "fsdp"), None, None),
            P("fsdp", None),
            P(),
        ),
        check_vma=False,
    )
```

time: 104 us -> 86 us (0.83)
  Pallas kernels: 94.7 us -> 80.3 us
  local copies, waits for them, and re-layouts: 6.36 us -> 3.26 us
    pallas_call x1, Pallas kernels: 94.7 us -> 80.3 us  [local(): call(*(pltpu.with_memory_space_constraint(v, pltpu.HBM) for v in operands))]
    unnamed x7 -> x3, local copies, waits for them, and re-layouts: 5.08 us -> 3.26 us
    reshape x1 -> x0, local copies, waits for them, and re-layouts: 1.29 us -> none  [local(): norm_gain.reshape(1, D)]
where the time goes in v2:
time: 86 us; the launch traced here: 85.9 us
  Pallas kernels  80.3 us (93%)
  local copies, waits for them, and re-layouts  3.26 us (4%)
  between operations  2.33 us (3%)
    pallas_call x1, Pallas kernels, local(): call(*(pltpu.with_memory_space_constraint(v, pltpu.HBM) for v in operands))  80.3 us
    unnamed x3, local copies, waits for them, and re-layouts  3.26 us

profile of v2, /device:TPU:1, one launch (start us, length us, event | category | flops | bytes accessed | tf_op | source)
XLA Modules:
  0.0 85.9 jit_solution(9367727154368390340)
XLA Ops:
  0.6 80.3 %balance.1 = (bf16[640,1536]{1,0:T(8,128)(2,1)S(1)}, bf16[640,1536]{1,0:T(8,128)(2,1)S(1)}, f32[48,1536]{1,0:T(8,128)S(1)}, f32[1,1]{1,0:T(1,128)}) custom-call(bf16[640,1536]{1,0:T(8,128)(2,1)} %bitcast.10, bf16[640,1536]{1,0:T(8,128)(2,1)} %bitcast.11, bf16[640,1536]{1,0:T(8,128)(2,1)} %bitcast.12, bf16[48,1536]{1,0:T(8,128)(2,1)} %w_hbm.1, ...), custom_call_target="tpu_custom_call" | custom-call | flops 9059999744 | bytes 10000000 | tf_op jit(solution)/shard_map/balance/pallas_call | solution.py:580
  81.0 1.3 %copy.16 = bf16[2,320,1536]{2,1,0:T(8,128)(2,1)} copy(bf16[2,320,1536]{2,1,0:T(8,128)(2,1)S(1)} %bitcast.9) | data formatting | bytes 3932160
  82.3 1.3 %copy.17 = bf16[2,320,1536]{2,1,0:T(8,128)(2,1)} copy(bf16[2,320,1536]{2,1,0:T(8,128)(2,1)S(1)} %bitcast.8) | data formatting | bytes 3932160
  83.5 0.7 copy.18

commit v3 on v2

--- a/solution.py
+++ b/solution.py
@@ -19,6 +19,7 @@
 SEQ = 320
 H = D // 2
 Q = D // 4
+QA, QB = 512, 256
 RB = 48
 
 Z_ARRIVE = (0, -1, 1, -2, 2, -3, 3, -4)
@@ -118,8 +119,6 @@
         sends = []
         if n == 0:
             sends = [("y", ("Ay", "L", 1, i)) for i in range(8)]
-        if n == 1:
-            sends = [("y", ("Ay", "S", 1, i)) for i in range(8)]
         ops.append(Op(("CA", n), sends=sends, cost=0.6, rank=2 + n))
     for i, zo in enumerate(Z_LEAVE):
         sends = []
@@ -129,7 +128,7 @@
             sends = [("z", ("Bz", "S", 1, j)) for j in range(4)]
         ops.append(Op(("CB", i), sends=sends, cost=0.35, rank=2 + i / 2))
     for i, off in enumerate(Z_LEAVE):
-        ops.append(Op(("FA", i), waits=[("Ay", "L", 1, i)], after=[("CA", 0), ("CA", 2)], sends=[("y", ("Ay", "L", 2, i))]))
+        ops.append(Op(("FA", i), waits=[("Ay", "L", 1, i)], after=[("CA", 0), ("CA", 1), ("CA", 2)], sends=[("y", ("Ay", "L", 2, i)), ("y", ("Ay", "S", 1, i))]))
         waits = [("Ay", "L", 2, i), ("Ay", "S", 1, i)]
         waits += [("Az", n) for n in {2: (4, 3), -2: (-3,), 0: (2, -2, 1, -1)}.get(off, ())]
         sends = [("z", ("Az", off))] if off else [("x", ("X", 0, k)) for k in range(3)]
@@ -162,10 +161,10 @@
     if event[0] in ("l1", "l2"):
         return 0.05
     if event[0] == "X":
-        return 1.1
+        return (0.73, 0.37)[event[1]]
     if event[0] == "G":
         return 0.15
-    return 0.4 * hops(event)
+    return (0.533 if event[0][0] == "A" else 0.267) * hops(event)
 
 
 GATHER = order(gather_ops(), size)
@@ -179,8 +178,8 @@
     rg_out, ag_out, wg_ref, loss_ref,
     wbuf, xb, ob, eb, ot, mixed, ss_ref, t_ref, g, gall,
     da, db, sa, ra, sa2, ra2, sb, rb, sb2, rb2,
-    xr, xg, my, mz, msg1, msg2, ls, lx, lmsg1, lmsg2, crow,
-    gain_in, gain_ref, len_ref, pid_ref, off_ref, prow_ref, gauge,
+    xra, xrb, xga, xgb, my, mz, msg1, msg2, ls, lx, lmsg1, lmsg2, crow,
+    gain_in, gain_ref, len_ref, pid_ref, off_ref, prow_ref, gauge_a, gauge_b,
     loc, g_send, g_recv, b_send, b_recv, o_send, o_recv, h_send, h_recv, r_recv,
     a_send, a2_send, s_send, s2_send, x_send, q_send, y_send, y_recv, z_send, z_recv, l_send, m_send,
 ):
@@ -256,7 +255,7 @@
             k = (0 if d == "D" else k - 1) if sender else k
             step = k if d == "S" else -k
             zz, yy = (zat(off), yat(step)) if kind == "Ay" else (zat(step), yat(off))
-        cols = pl.ds(0, Q) if kind[0] == "A" else pl.ds(Q, Q)
+        cols = pl.ds(0, QA) if kind[0] == "A" else pl.ds(QA, QB)
         return wbuf.at[c, zz, yy, :, cols]
 
     def turn(n):
@@ -282,7 +281,7 @@
             loads[2].wait()
         if step in turn_at:
             turn(turn_at[step])
-    for part in range(2):
+    for part, gauge in enumerate((gauge_a, gauge_b)):
         remote(gauge, gauge, b_send.at[part], b_recv.at[part], sibling).wait_recv()
     for copy in loads[3:]:
         copy.wait()
@@ -345,7 +344,7 @@
     for k in range(7):
         start(remote(msg2, mz.at[k], z_send.at[k], z_recv.at[k], dev(x, c, zs[k], y)))
     lax.fori_loop(4, 10, prepare, 0)
-    for part in range(2):
+    for part, gauge in enumerate((gauge_a, gauge_b)):
         remote(gauge, gauge, g_send.at[part], g_recv.at[0], sibling).wait_send()
         remote(gauge, gauge, b_send.at[part], g_recv.at[0], sibling).wait_send()
     for k in range(7):
@@ -395,11 +394,13 @@
         src[...] = value.astype(BF16)
         remote(src, dst, sem.at[0], r_recv.at[S_ID[event]], peer(event, SCATTER_TO)).start()
 
+    xr, xg = (xra, xrb), (xga, xgb)
+
     def got_of(event):
         if event[0] == "X":
-            return xr.at[event[1], lax.rem(x + NX - 1 - event[2], NX)]
+            return xr[event[1]].at[lax.rem(x + NX - 1 - event[2], NX)]
         if event[0] == "G":
-            return xg.at[1 - c, event[1]]
+            return xg[event[1]].at[1 - c]
         if event[0] == "l1":
             return ls
         if event[0] == "l2":
@@ -407,9 +408,9 @@
         return slot(event)[1]
 
     def spread(ab, value):
-        xr[ab, x] = value
+        xr[ab][x] = value.astype(BF16)
         for k in range(3):
-            blk = xr.at[ab, x]
+            blk = xr[ab].at[x]
             remote(blk, blk, x_send.at[ab], r_recv.at[S_ID["X", ab, k]], dev(xs[k], c, z, y)).start()
 
     for op in SCATTER:
@@ -423,17 +424,18 @@
         if kind == "CA":
             yy = yat(Y_LEAVE[op.key[1]])
             lhs = ot[:, yy].reshape(8 * RB, 2 * TOK)
-            da[:, yy] = jnp.dot(lhs, gall[:, 0:Q], preferred_element_type=F32).reshape(8, RB, Q)
+            da[:, yy] = jnp.dot(lhs, gall[:, 0:QA], preferred_element_type=F32).reshape(8, RB, QA)
             for axis, event in op.sends:
                 push(event, da[zat(Z_LEAVE[event[3]]), yy])
         elif kind == "CB":
             zz = zat(Z_LEAVE[op.key[1]])
             lhs = ot[zz].reshape(4 * RB, 2 * TOK)
-            db[zz] = jnp.dot(lhs, gall[:, Q:H], preferred_element_type=F32).reshape(4, RB, Q)
+            db[zz] = jnp.dot(lhs, gall[:, QA:H], preferred_element_type=F32).reshape(4, RB, QB)
             for axis, event in op.sends:
                 push(event, db[zz, yat(Y_LEAVE[event[3]])])
         elif kind == "FA":
             push(op.sends[0][1], da[zat(Z_LEAVE[op.key[1]]), yat(1)] + got)
+            push(op.sends[1][1], da[zat(Z_LEAVE[op.key[1]]), yat(-1)])
         elif kind == "TA":
             value = da[zat(Z_LEAVE[op.key[1]]), y] + got
             if Z_LEAVE[op.key[1]]:
@@ -448,14 +450,15 @@
                 spread(1, value)
         elif kind == "X":
             ab = op.key[1]
-            value = ((xr[ab, 0] + xr[ab, 1]) + (xr[ab, 2] + xr[ab, 3])) * (1.0 / 512.0)
-            xg[c, ab] = value
-            blk = xg.at[c, ab]
+            part = [xr[ab][n].astype(F32) for n in range(NX)]
+            value = ((part[0] + part[1]) + (part[2] + part[3])) * (1.0 / 512.0)
+            xg[ab][c] = value
+            blk = xg[ab].at[c]
             start(remote(blk, blk, q_send.at[ab], r_recv.at[S_ID["G", ab]], sibling))
         elif kind == "W":
             ab = op.key[1]
             for h in range(2):
-                wg_ref[:, pl.ds(h * H + ab * Q, Q)] = xg[h, ab]
+                wg_ref[:, pl.ds(h * H + ab * QA, (QA, QB)[ab])] = xg[ab][h]
         elif kind == "pair":
             pair = lmsg1[...] + ls[...]
             lmsg2[...] = pair
@@ -487,7 +490,7 @@
     for ref, sem in ((sa, a_send), (sa2, a2_send), (sb, s_send), (sb2, s2_send)):
         remote(ref, ref, sem.at[0], r_recv.at[0], sibling).wait_send()
     for ab in range(2):
-        ref = xr.at[ab, 0:3]
+        ref = xr[ab].at[0:3]
         remote(ref, ref, x_send.at[ab], r_recv.at[0], sibling).wait_send()
     for copy in sent:
         copy.wait_send()
@@ -513,18 +516,20 @@
         pltpu.VMEM((TOK, 128), F32),
         pltpu.VMEM((2, TOK, H), BF16),
         pltpu.VMEM((2 * TOK, H), BF16),
-        pltpu.VMEM((NZ, NY, RB, Q), F32),
-        pltpu.VMEM((NZ, NY, RB, Q), F32),
-        pltpu.VMEM((3, 8, RB, Q), BF16),
-        pltpu.VMEM((3, 8, RB, Q), BF16),
-        pltpu.VMEM((7, RB, Q), BF16),
-        pltpu.VMEM((7, RB, Q), BF16),
-        pltpu.VMEM((7, 4, RB, Q), BF16),
-        pltpu.VMEM((7, 4, RB, Q), BF16),
-        pltpu.VMEM((3, RB, Q), BF16),
-        pltpu.VMEM((3, RB, Q), BF16),
-        pltpu.VMEM((2, 4, RB, Q), F32),
-        pltpu.VMEM((2, 2, RB, Q), F32),
+        pltpu.VMEM((NZ, NY, RB, QA), F32),
+        pltpu.VMEM((NZ, NY, RB, QB), F32),
+        pltpu.VMEM((3, 8, RB, QA), BF16),
+        pltpu.VMEM((3, 8, RB, QA), BF16),
+        pltpu.VMEM((7, RB, QA), BF16),
+        pltpu.VMEM((7, RB, QA), BF16),
+        pltpu.VMEM((7, 4, RB, QB), BF16),
+        pltpu.VMEM((7, 4, RB, QB), BF16),
+        pltpu.VMEM((3, RB, QB), BF16),
+        pltpu.VMEM((3, RB, QB), BF16),
+        pltpu.VMEM((4, RB, QA), BF16),
+        pltpu.VMEM((4, RB, QB), BF16),
+        pltpu.VMEM((2, RB, QA), F32),
+        pltpu.VMEM((2, RB, QB), F32),
         pltpu.VMEM((3, 8, 128), F32),
         pltpu.VMEM((7, 8, 128), F32),
         pltpu.VMEM((8, 128), F32),
@@ -540,7 +545,8 @@
         pltpu.SMEM((512,), jnp.int32),
         pltpu.SMEM((512,), F32),
         pltpu.VMEM((4, 128), jnp.int32),
-        pltpu.VMEM((31, RB, Q), BF16),
+        pltpu.VMEM((31, RB, QA), BF16),
+        pltpu.VMEM((31, RB, QB), BF16),
         dma((10,)),
         dma((2,)), dma((n_g,)), dma((2,)), dma((2,)),
         dma((4,)), dma((4,)), dma((1,)), dma((1,)),

time: 86 us -> 82.7 us (0.962)
  Pallas kernels: 80.3 us -> 77 us
    pallas_call x1, Pallas kernels: 80.3 us -> 77 us  [local(): call(*(pltpu.with_memory_space_constraint(v, pltpu.HBM) for v in operands))]
where the time goes in v3:
time: 82.7 us; the launch traced here: 82.6 us
  Pallas kernels  77 us (93%)
  local copies, waits for them, and re-layouts  3.26 us (4%)
  between operations  2.33 us (3%)
    pallas_call x1, Pallas kernels, local(): call(*(pltpu.with_memory_space_constraint(v, pltpu.HBM) for v in operands))  77 us
    unnamed x3, local copies, waits for them, and re-layouts  3.26 us

profile of v3, /device:TPU:1, one launch (start us, length us, event | category | flops | bytes accessed | tf_op | source)
XLA Modules:
  0.0 82.6 jit_solution(2798181977481372845)
XLA Ops:
  0.6 77.0 %balance.1 = (bf16[640,1536]{1,0:T(8,128)(2,1)S(1)}, bf16[640,1536]{1,0:T(8,128)(2,1)S(1)}, f32[48,1536]{1,0:T(8,128)S(1)}, f32[1,1]{1,0:T(1,128)}) custom-call(bf16[640,1536]{1,0:T(8,128)(2,1)} %bitcast.10, bf16[640,1536]{1,0:T(8,128)(2,1)} %bitcast.11, bf16[640,1536]{1,0:T(8,128)(2,1)} %bitcast.12, bf16[48,1536]{1,0:T(8,128)(2,1)} %w_hbm.1, ...), custom_call_target="tpu_custom_call" | custom-call | flops 9059999744 | bytes 10000000 | tf_op jit(solution)/shard_map/balance/pallas_call | solution.py:586
  77.7 1.3 %copy.16 = bf16[2,320,1536]{2,1,0:T(8,128)(2,1)} copy(bf16[2,320,1536]{2,1,0:T(8,128)(2,1)S(1)} %bitcast.9) | data formatting | bytes 3932160
  78.9 1.3 %copy.17 = bf16[2,320,1536]{2,1,0:T(8,128)(2,1)} copy(bf16[2,320,1536]{2,1,0:T(8,128)(2,1)S(1)} %bitcast.8) | data formatting | bytes 3932160
  80.2 0.7 copy.18

commit v4 on v3

--- a/solution.py
+++ b/solution.py
@@ -29,7 +29,7 @@
 
 
 class Op:
-    def __init__(self, key, waits=(), after=(), sends=(), cost=0.1, rank=0):
+    def __init__(self, key, waits=(), after=(), sends=(), cost=0.2, rank=0):
         self.key, self.waits, self.after, self.sends, self.cost, self.rank = key, waits, after, sends, cost, rank
 
 
@@ -49,7 +49,7 @@
         now = ready + op.cost
         for axis, event in op.sends:
             free[axis] = max(now, free.get(axis, 0.0)) + size(event)
-            at[event] = free[axis] + (0.9 if axis == "s" else 2.0 if size(event) > 0.5 else 1.6)
+            at[event] = free[axis] + (0.9 if axis == "s" else 3.2 if size(event) > 0.6 else 2.8)
         done.add(op.key)
         out.append(op)
     return out
@@ -107,7 +107,7 @@
     return ops
 
 
-LATE = (-3, 3, -4)
+LATE = (-2, 2, -3, 3, -4)
 
 
 def scatter_ops():
@@ -289,9 +289,9 @@
     gain_ref[...] = jnp.concatenate([wide[n : n + 1] for n in range(D // 128)], axis=1)
 
     def forward(m, _):
-        rows = pl.ds(pl.multiple_of(m * 160, 160), 160)
-        ss = jnp.zeros((160, 1), F32)
-        tt = jnp.zeros((160, 1), F32)
+        rows = pl.ds(pl.multiple_of(m * 320, 320), 320)
+        ss = jnp.zeros((320, 1), F32)
+        tt = jnp.zeros((320, 1), F32)
         for h in range(2):
             cols = pl.ds(h * H, H)
             w = wbuf[h].reshape(D, H)
@@ -300,11 +300,11 @@
             eg = eb[rows, cols].astype(F32) * gain_ref[:, cols]
             ss = ss + jnp.sum(acc * acc, axis=1, keepdims=True)
             tt = tt + jnp.sum(acc * eg, axis=1, keepdims=True)
-        ss_ref[rows, :] = jnp.broadcast_to(ss, (160, 128))
-        t_ref[rows, :] = jnp.broadcast_to(tt, (160, 128))
+        ss_ref[rows, :] = jnp.broadcast_to(ss, (320, 128))
+        t_ref[rows, :] = jnp.broadcast_to(tt, (320, 128))
         return 0
 
-    lax.fori_loop(0, TOK // 160, forward, 0)
+    lax.fori_loop(0, TOK // 320, forward, 0)
 
     first = (gi * 32 + fi) * 2
     lane = lax.broadcasted_iota(jnp.int32, (8, 128), 1)
@@ -368,12 +368,20 @@
         return 0
 
     lax.fori_loop(0, TOK // 64, gradient, 0)
-    start(remote(g.at[1 - c], gall.at[pl.ds(TOK, TOK)], h_send.at[0], h_recv.at[0], sibling))
+    pieces = (pl.ds(0, QA), pl.ds(QA, QB))
+    for n, cols in enumerate(pieces):
+        theirs = gall.at[pl.ds(TOK, TOK), cols]
+        start(remote(g.at[1 - c, :, cols], theirs, h_send.at[n], h_recv.at[n], sibling))
     for n in range(4):
         theirs = ot.at[2 * n : 2 * n + 2, :, :, TOK : 2 * TOK]
         remote(theirs, theirs, o_send.at[n], o_recv.at[n], sibling).wait_recv()
-    theirs = gall.at[pl.ds(TOK, TOK)]
-    remote(theirs, theirs, h_send.at[0], h_recv.at[0], sibling).wait_recv()
+    taken = set()
+
+    def take(n):
+        if n not in taken:
+            taken.add(n)
+            theirs = gall.at[pl.ds(TOK, TOK), pieces[n]]
+            remote(theirs, theirs, h_send.at[n], h_recv.at[n], sibling).wait_recv()
 
     def slot(event):
         kind, d = event[:2]
@@ -422,12 +430,14 @@
                 got = got + dst[...].astype(F32)
         kind = op.key[0] if isinstance(op.key, tuple) else op.key
         if kind == "CA":
+            take(0)
             yy = yat(Y_LEAVE[op.key[1]])
             lhs = ot[:, yy].reshape(8 * RB, 2 * TOK)
             da[:, yy] = jnp.dot(lhs, gall[:, 0:QA], preferred_element_type=F32).reshape(8, RB, QA)
             for axis, event in op.sends:
                 push(event, da[zat(Z_LEAVE[event[3]]), yy])
         elif kind == "CB":
+            take(1)
             zz = zat(Z_LEAVE[op.key[1]])
             lhs = ot[zz].reshape(4 * RB, 2 * TOK)
             db[zz] = jnp.dot(lhs, gall[:, QA:H], preferred_element_type=F32).reshape(4, RB, QB)
@@ -549,7 +559,7 @@
         pltpu.VMEM((31, RB, QB), BF16),
         dma((10,)),
         dma((2,)), dma((n_g,)), dma((2,)), dma((2,)),
-        dma((4,)), dma((4,)), dma((1,)), dma((1,)),
+        dma((4,)), dma((4,)), dma((2,)), dma((2,)),
         dma((n_s,)),
         dma((1,)), dma((1,)), dma((1,)), dma((1,)), dma((2,)), dma((2,)),
         dma((3,)), dma((3,)), dma((7,)), dma((7,)),

time: 82.7 us -> 79.9 us (0.966)
  Pallas kernels: 77 us -> 74.2 us
    pallas_call x1, Pallas kernels: 77 us -> 74.2 us  [local(): call(*(pltpu.with_memory_space_constraint(v, pltpu.HBM) for v in operands))]
where the time goes in v4:
time: 79.9 us; the launch traced here: 79.8 us
  Pallas kernels  74.2 us (93%)
  local copies, waits for them, and re-layouts  3.26 us (4%)
  between operations  2.33 us (3%)
    pallas_call x1, Pallas kernels, local(): call(*(pltpu.with_memory_space_constraint(v, pltpu.HBM) for v in operands))  74.2 us
    unnamed x3, local copies, waits for them, and re-layouts  3.26 us

profile of v4, /device:TPU:1, one launch (start us, length us, event | category | flops | bytes accessed | tf_op | source)
XLA Modules:
  0.0 79.8 jit_solution(16258952649869827688)
XLA Ops:
  0.6 74.2 %balance.1 = (bf16[640,1536]{1,0:T(8,128)(2,1)S(1)}, bf16[640,1536]{1,0:T(8,128)(2,1)S(1)}, f32[48,1536]{1,0:T(8,128)S(1)}, f32[1,1]{1,0:T(1,128)}) custom-call(bf16[640,1536]{1,0:T(8,128)(2,1)} %bitcast.10, bf16[640,1536]{1,0:T(8,128)(2,1)} %bitcast.11, bf16[640,1536]{1,0:T(8,128)(2,1)} %bitcast.12, bf16[48,1536]{1,0:T(8,128)(2,1)} %w_hbm.1, ...), custom_call_target="tpu_custom_call" | custom-call | flops 9059999744 | bytes 10000000 | tf_op jit(solution)/shard_map/balance/pallas_call | solution.py:596
  74.9 1.3 %copy.16 = bf16[2,320,1536]{2,1,0:T(8,128)(2,1)} copy(bf16[2,320,1536]{2,1,0:T(8,128)(2,1)S(1)} %bitcast.9) | data formatting | bytes 3932160
  76.1 1.3 %copy.17 = bf16[2,320,1536]{2,1,0:T(8,128)(2,1)} copy(bf16[2,320,1536]{2,1,0:T(8,128)(2,1)S(1)} %bitcast.8) | data formatting | bytes 3932160
  77.4 0.7 copy.18

commit v5 on v4

--- a/solution.py
+++ b/solution.py
@@ -153,7 +153,7 @@
     ops.append(Op("pair", waits=[("l1",)], sends=[("x", ("l2", k)) for k in range(3)]))
     ops.append(Op("total", waits=[("l2", k) for k in range(3)]))
     for n in range(4):
-        ops.append(Op(("attn", n), after=[("CA", 3), ("CB", 7)], cost=1.2, rank=30 + n))
+        ops.append(Op(("attn", n), after=[("TA", 7), ("FB", 7, 3)], cost=1.2, rank=30 + n))
     return ops
 
 

time: 79.9 us -> 79.6 us (level)
  no operation moved by 1% of the time
where the time goes in v5:
time: 79.6 us; the launch traced here: 79.5 us
  Pallas kernels  73.9 us (93%)
  local copies, waits for them, and re-layouts  3.26 us (4%)
  between operations  2.33 us (3%)
    pallas_call x1, Pallas kernels, local(): call(*(pltpu.with_memory_space_constraint(v, pltpu.HBM) for v in operands))  73.9 us
    unnamed x3, local copies, waits for them, and re-layouts  3.26 us

profile of v5, /device:TPU:1, one launch (start us, length us, event | category | flops | bytes accessed | tf_op | source)
XLA Modules:
  0.0 79.5 jit_solution(15334623314461113783)
XLA Ops:
  0.6 73.9 %balance.1 = (bf16[640,1536]{1,0:T(8,128)(2,1)S(1)}, bf16[640,1536]{1,0:T(8,128)(2,1)S(1)}, f32[48,1536]{1,0:T(8,128)S(1)}, f32[1,1]{1,0:T(1,128)}) custom-call(bf16[640,1536]{1,0:T(8,128)(2,1)} %bitcast.10, bf16[640,1536]{1,0:T(8,128)(2,1)} %bitcast.11, bf16[640,1536]{1,0:T(8,128)(2,1)} %bitcast.12, bf16[48,1536]{1,0:T(8,128)(2,1)} %w_hbm.1, ...), custom_call_target="tpu_custom_call" | custom-call | flops 9059999744 | bytes 10000000 | tf_op jit(solution)/shard_map/balance/pallas_call | solution.py:596
  74.6 1.3 %copy.16 = bf16[2,320,1536]{2,1,0:T(8,128)(2,1)} copy(bf16[2,320,1536]{2,1,0:T(8,128)(2,1)S(1)} %bitcast.9) | data formatting | bytes 3932160
  75.8 1.3 %copy.17 = bf16[2,320,1536]{2,1,0:T(8,128)(2,1)} copy(bf16[2,320,1536]{2,1,0:T(8,128)(2,1)S(1)} %bitcast.8) | data formatting | bytes 3932160
  77.1 0.7 copy.18
